TPU v7x, 256 devices: a whole 4x4x8 slice. The times are simulated.
256 devices in a mesh: fsdp: 128 (over x_lo, z, y, core), dp: 2 (over x_hi).
Axes of the slice: x: 4 (x_hi: 2, x_lo: 2; x = x_hi * 2 + x_lo), y: 4, z: 8, core: 2. Of those that a mesh axis runs over, the one named last changes fastest.
Arguments:
- inputs: bfloat16 [512, 256, 512], P(('fsdp', 'dp')), may hold values from -6 to 6
- memory: bfloat16 [512, 256, 512], P(('fsdp', 'dp')), may hold values from -6 to 6
- out_grad: bfloat16 [512, 256, 512], P(('fsdp', 'dp')), may hold values from -6 to 6
- weights: float32 [8192, 512], P('fsdp'), may hold values from -0.1659025 to 0.1659025
- first_moment: float32 [8192, 512], P('fsdp'), may hold values from -94.130055 to 94.130055
- second_moment: float32 [8192, 512], P('fsdp'), may hold values from 0 to 27525.12, as said below
- norms: float32 [6, 512], P(None, 'fsdp'), may hold values from -0.3 to 1.4
- norm_first: float32 [6, 512], P(None, 'fsdp'), may hold values from -123.09315 to 123.09315
- norm_second: float32 [6, 512], P(None, 'fsdp'), may hold values from 0 to 47185.92, as said below
Outputs:
- outputs: bfloat16 [512, 256, 512], P(('fsdp', 'dp'))
- grad_inputs: float32 [512, 256, 512], P(('fsdp', 'dp'))
- grad_memory: float32 [512, 256, 512], P(('fsdp', 'dp'))
- weight_grads: float32 [8192, 512], P('fsdp')
- new_weights: float32 [8192, 512], P('fsdp')
- new_second: float32 [8192, 512], P('fsdp')
- norm_grads: float32 [6, 512], P(None, 'fsdp')
- new_norms: float32 [6, 512], P(None, 'fsdp')
- new_norm_second: float32 [6, 512], P(None, 'fsdp')
Inputs may be any that keep to these rules, and one draw needn't show every extreme that they name: `second_moment`: positive. `norm_second`: positive.
All inputs are finite; a program needn't handle non-finite values.
Results may differ from a plain program's by a relative error of at most 0.034.
The roundings to bfloat16 on the way count: a program that leaves them out, or rounds other values in their place, can miss the bound.
Values may be sent and summed in bfloat16 or wider, within the bound.
No kernel may reach another device: no remote copies, remote signals or barrier semaphores. Data moves between devices by JAX's collectives and lax.ppermute only.
A program may use at most 192 MiB of HBM per device.

v0:
```python
import jax
import jax.numpy as jnp
from jax import lax
from jax.sharding import PartitionSpec as P

HEADS = 8
STEP = 10


EPS_NORM = 1e-05
BETA_ONE = 0.9
BETA_TWO = 0.98
RATE = 0.1
RATE_NORM = 0.4
DECAY = 0.01
EPS_ADAM = 1e-09


def product(former, latter):
    return jnp.dot(former, latter, preferred_element_type=jnp.float32)


def left_product(former, latter):
    return lax.dot_general(
        former, latter, (((0,), (0,)), ((), ())), preferred_element_type=jnp.float32
    )


def right_product(former, latter):
    return lax.dot_general(
        former, latter, (((1,), (1,)), ((), ())), preferred_element_type=jnp.float32
    )


def layer_norm(vector, gain_row, shift_row):
    centre = vector - jnp.mean(vector, axis=-1, keepdims=True)
    factor = lax.rsqrt(jnp.mean(centre * centre, axis=-1, keepdims=True) + EPS_NORM)
    normed = centre * factor
    return (normed * gain_row + shift_row, normed, factor)


def norm_back(grad_out, normed, factor, gain_row):
    scaled = grad_out * gain_row
    mean_one = jnp.mean(scaled, axis=-1, keepdims=True)
    mean_two = jnp.mean(scaled * normed, axis=-1, keepdims=True)
    grad_in = factor * (scaled - mean_one - normed * mean_two)
    return (grad_in, jnp.sum(grad_out * normed, axis=0), jnp.sum(grad_out, axis=0))


def split_heads(vector):
    return vector.reshape(vector.shape[0], HEADS, vector.shape[1] // HEADS)


def attention_scores(queries, key_rows):
    factor = (queries.shape[1] // HEADS) ** (-0.5)
    return (
        jnp.einsum(
            "qhe,khe->hqk",
            split_heads(queries),
            split_heads(key_rows),
            preferred_element_type=jnp.float32,
        )
        * factor
    )


def attend_forward(queries, key_rows, values):
    scores = attention_scores(queries, key_rows)
    highest = jnp.max(scores, axis=-1, keepdims=True)
    raised = jnp.exp(scores - highest)
    summed = jnp.sum(raised, axis=-1, keepdims=True)
    soft_low = (raised / summed).astype(jnp.bfloat16)
    mixture = jnp.einsum(
        "hqk,khe->qhe", soft_low, split_heads(values), preferred_element_type=jnp.float32
    )
    return (mixture.reshape(queries.shape).astype(jnp.bfloat16), highest + jnp.log(summed))


def attend_back(queries, key_rows, values, log_total, grad_mix):
    factor = (queries.shape[1] // HEADS) ** (-0.5)
    scores = attention_scores(queries, key_rows)
    softmax_rows = jnp.exp(scores - log_total)
    heads_grad = split_heads(grad_mix)
    grad_values = jnp.einsum(
        "hqk,qhe->khe",
        softmax_rows.astype(jnp.bfloat16),
        heads_grad,
        preferred_element_type=jnp.float32,
    )
    grad_soft = jnp.einsum(
        "qhe,khe->hqk", heads_grad, split_heads(values), preferred_element_type=jnp.float32
    )
    inner = jnp.sum(softmax_rows * grad_soft, axis=-1, keepdims=True)
    grad_scores = (softmax_rows * (grad_soft - inner)).astype(jnp.bfloat16)
    grad_query = (
        jnp.einsum(
            "hqk,khe->qhe", grad_scores, split_heads(key_rows), preferred_element_type=jnp.float32
        )
        * factor
    )
    grad_keys = (
        jnp.einsum(
            "hqk,qhe->khe", grad_scores, split_heads(queries), preferred_element_type=jnp.float32
        )
        * factor
    )
    return (
        grad_query.reshape(queries.shape).astype(jnp.bfloat16),
        grad_keys.reshape(key_rows.shape).astype(jnp.bfloat16),
        grad_values.reshape(values.shape).astype(jnp.bfloat16),
    )


def unpack(full_w, model_width):
    hidden = (full_w.shape[0] - 8 * model_width) // 2
    matrices = [full_w[block * model_width : (block + 1) * model_width] for block in range(8)]
    w_in = full_w[8 * model_width : 8 * model_width + hidden]
    w_down = full_w[8 * model_width + hidden :]
    return (matrices, w_in, w_down)


def forward_pass(inputs_row, memory_row, full_w, full_n):
    matrices, w_in, w_down = unpack(full_w, inputs_row.shape[1])
    norm_rows = full_n.astype(jnp.float32)
    block_input = inputs_row.astype(jnp.float32)
    stored = {}
    normal_one, stored["normed_one"], stored["factor_one"] = layer_norm(
        block_input, norm_rows[0], norm_rows[1]
    )
    first_in = normal_one.astype(jnp.bfloat16)
    stored["first_in"] = first_in
    stored["query_one"] = product(first_in, matrices[0]).astype(jnp.bfloat16)
    stored["key_one"] = product(first_in, matrices[1]).astype(jnp.bfloat16)
    stored["value_one"] = product(first_in, matrices[2]).astype(jnp.bfloat16)
    stored["mix_one"], stored["log_one"] = attend_forward(
        stored["query_one"], stored["key_one"], stored["value_one"]
    )
    after_one = block_input + product(stored["mix_one"], matrices[3])
    normal_two, stored["normed_two"], stored["factor_two"] = layer_norm(
        after_one, norm_rows[2], norm_rows[3]
    )
    second_in = normal_two.astype(jnp.bfloat16)
    stored["second_in"] = second_in
    stored["query_two"] = product(second_in, matrices[4]).astype(jnp.bfloat16)
    stored["key_two"] = product(memory_row, matrices[5]).astype(jnp.bfloat16)
    stored["value_two"] = product(memory_row, matrices[6]).astype(jnp.bfloat16)
    stored["mix_two"], stored["log_two"] = attend_forward(
        stored["query_two"], stored["key_two"], stored["value_two"]
    )
    after_two = after_one + product(stored["mix_two"], matrices[7])
    normal_three, stored["normed_three"], stored["factor_three"] = layer_norm(
        after_two, norm_rows[4], norm_rows[5]
    )
    third_in = normal_three.astype(jnp.bfloat16)
    stored["third_in"] = third_in
    up_proj = right_product(third_in, w_in)
    stored["up_proj"] = up_proj
    active = jax.nn.silu(up_proj).astype(jnp.bfloat16)
    stored["active"] = active
    result = after_two + product(active, w_down)
    return (stored, result)


def backward_pass(stored, grad_low, memory_row, full_w, full_n):
    matrices, w_in, w_down = unpack(full_w, grad_low.shape[1])
    norm_rows = full_n.astype(jnp.float32)
    grad_out = grad_low.astype(jnp.float32)
    grad_down = left_product(stored["active"], grad_low)
    grad_act = right_product(grad_low, w_down)
    up_proj = stored["up_proj"]
    sigma = jax.nn.sigmoid(up_proj)
    grad_up = (grad_act * sigma * (1.0 + up_proj * (1.0 - sigma))).astype(jnp.bfloat16)
    grad_inw = left_product(grad_up, stored["third_in"])
    back_three, gain_three, bias_three = norm_back(
        product(grad_up, w_in), stored["normed_three"], stored["factor_three"], norm_rows[4]
    )
    grad_two = grad_out + back_three
    cross_out = grad_two.astype(jnp.bfloat16)
    grad_woc = left_product(stored["mix_two"], cross_out)
    cross_mix = right_product(cross_out, matrices[7]).astype(jnp.bfloat16)
    grad_qc, grad_kc, grad_vc = attend_back(
        stored["query_two"], stored["key_two"], stored["value_two"], stored["log_two"], cross_mix
    )
    grad_wqc = left_product(stored["second_in"], grad_qc)
    grad_wkc = left_product(memory_row, grad_kc)
    grad_wvc = left_product(memory_row, grad_vc)
    grad_memory = right_product(grad_kc, matrices[5]) + right_product(grad_vc, matrices[6])
    back_two, gain_two, bias_two = norm_back(
        right_product(grad_qc, matrices[4]),
        stored["normed_two"],
        stored["factor_two"],
        norm_rows[2],
    )
    grad_one = grad_two + back_two
    self_out = grad_one.astype(jnp.bfloat16)
    grad_wo = left_product(stored["mix_one"], self_out)
    self_mix = right_product(self_out, matrices[3]).astype(jnp.bfloat16)
    grad_q, grad_k, grad_v = attend_back(
        stored["query_one"], stored["key_one"], stored["value_one"], stored["log_one"], self_mix
    )
    grad_wq = left_product(stored["first_in"], grad_q)
    grad_wk = left_product(stored["first_in"], grad_k)
    grad_wv = left_product(stored["first_in"], grad_v)
    grad_first = (
        right_product(grad_q, matrices[0])
        + right_product(grad_k, matrices[1])
        + right_product(grad_v, matrices[2])
    )
    back_one, gain_one, bias_one = norm_back(
        grad_first, stored["normed_one"], stored["factor_one"], norm_rows[0]
    )
    grad_start = grad_one + back_one
    weight_term = jnp.concatenate(
        [
            grad_wq,
            grad_wk,
            grad_wv,
            grad_wo,
            grad_wqc,
            grad_wkc,
            grad_wvc,
            grad_woc,
            grad_inw,
            grad_down,
        ],
        axis=0,
    )
    norm_term = jnp.stack([gain_one, bias_one, gain_two, bias_two, gain_three, bias_three])
    return (grad_start, grad_memory, weight_term, norm_term)


def adam_update(param, first, second, grad, rate):
    first_new = BETA_ONE * first + (1.0 - BETA_ONE) * grad
    second_new = BETA_TWO * second + (1.0 - BETA_TWO) * grad * grad
    fix_one = 1.0 - BETA_ONE**STEP
    fix_two = 1.0 - BETA_TWO**STEP
    update = first_new / fix_one / (jnp.sqrt(second_new / fix_two) + EPS_ADAM)
    return (param - rate * (update + DECAY * param), second_new)


def local(
    inputs, memory, out_grad, weights, first_moment, second_moment, norms, norm_first, norm_second
):
    shards = (weights.astype(jnp.bfloat16), norms.astype(jnp.bfloat16))
    group_size = lax.axis_size("fsdp")
    grad_w = jnp.zeros((weights.shape[0] * group_size, weights.shape[1]), jnp.float32)
    grad_n = jnp.zeros((norms.shape[0], norms.shape[1] * group_size), jnp.float32)
    results = []
    grads_start = []
    grads_memory = []
    for sentence in range(inputs.shape[0]):
        full_w, full_n = (
            lax.all_gather(shards[0], "fsdp", axis=0, tiled=True),
            lax.all_gather(shards[1], "fsdp", axis=1, tiled=True),
        )
        stored, result = forward_pass(inputs[sentence], memory[sentence], full_w, full_n)
        full_w, full_n = (
            lax.all_gather(shards[0], "fsdp", axis=0, tiled=True),
            lax.all_gather(shards[1], "fsdp", axis=1, tiled=True),
        )
        grad_start, grad_mem, weight_term, norm_term = backward_pass(
            stored, out_grad[sentence], memory[sentence], full_w, full_n
        )
        results.append(result)
        grads_start.append(grad_start)
        grads_memory.append(grad_mem)
        grad_w = grad_w + weight_term
        grad_n = grad_n + norm_term
    owned_w, owned_n = (
        lax.psum_scatter(grad_w, "fsdp", scatter_dimension=0, tiled=True),
        lax.psum_scatter(grad_n, "fsdp", scatter_dimension=1, tiled=True),
    )
    owned_w, owned_n = (
        lax.psum(owned_w.astype(jnp.bfloat16), "dp").astype(jnp.float32),
        lax.psum(owned_n.astype(jnp.bfloat16), "dp").astype(jnp.float32),
    )
    new_w, second_w = adam_update(weights, first_moment, second_moment, owned_w, RATE)
    new_n, second_n = adam_update(norms, norm_first, norm_second, owned_n, RATE_NORM)
    outputs = jnp.stack(results).astype(jnp.bfloat16)
    return (
        outputs,
        jnp.stack(grads_start),
        jnp.stack(grads_memory),
        owned_w,
        new_w,
        second_w,
        owned_n,
        new_n,
        second_n,
    )


def solution(mesh):
    return jax.shard_map(
        local,
        mesh=mesh,
        in_specs=(
            P(("fsdp", "dp"), None, None),
            P(("fsdp", "dp"), None, None),
            P(("fsdp", "dp"), None, None),
            P("fsdp", None),
            P("fsdp", None),
            P("fsdp", None),
            P(None, "fsdp"),
            P(None, "fsdp"),
            P(None, "fsdp"),
        ),
        out_specs=(
            P(("fsdp", "dp"), None, None),
            P(("fsdp", "dp"), None, None),
            P(("fsdp", "dp"), None, None),
            P("fsdp", None),
            P("fsdp", None),
            P("fsdp", None),
            P(None, "fsdp"),
            P(None, "fsdp"),
            P(None, "fsdp"),
        ),
        check_vma=False,
    )
```

profile of v0, /device:TPU:2, one launch (start us, length us, event | category | flops | bytes accessed | tf_op | source)
XLA Modules:
  0.0 996.8 jit_solution(5014467420487923922)
XLA Ops:
  7.2 1.6 convert_element_type.358
  9.6 159.1 %all-gather = bf16[128,4,6]{2,1,0:T(4,128)(2,1)S(1)} all-gather(bf16[1,4,6]{2,1,0:T(4,128)(2,1)S(1)} %convert_bitcast_fusion.2), channel_id=1, replica_groups=mesh['fsdp'=128,'dp'=2] {'fsdp'}, dimensions={0}, use_global_device_ids=true | all-gather | bytes 6192 | tf_op jit(solution)/shard_map/all_gather | solution.py:254
  168.8 1.2 convert_reduce_fusion.1
  170.0 1.3 fusion.92
  171.4 61.8 %all-gather.3.cloned.1.call-done = bf16[8192,512]{1,0:T(8,128)(2,1)} async-done(((bf16[64,512]{1,0:T(8,128)(2,1)}), bf16[8192,512]{1,0:T(8,128)(2,1)}) %all-gather.3.cloned.1.call-update) | async-done | bytes 8388624 | tf_op jit(solution)/shard_map/all_gather | solution.py:253
  233.2 1.5 convolution_convert_fusion.22
  234.8 1.5 convolution_convert_fusion.21
  237.2 1.4 convolution_convert_fusion.14
  238.7 1.5 convolution_convert_fusion.13
  240.4 1.5 convolution_convert_fusion.15
  242.8 1.4 convolution_convert_fusion.23
  245.1 1.3 convolution_convert_fusion.11
  247.2 1.3 convolution_convert_fusion.9
  249.4 1.3 convolution_convert_fusion.17
  251.6 1.3 convolution_convert_fusion.19
  256.0 1.4 fusion.206
  257.7 2.1 convolution_convert_fusion.10
  259.8 1.8 copy.120
  261.6 1.6 multiply_reduce_fusion.4
  264.5 1.6 fusion.207
  269.4 1.5 fusion.208
  271.7 2.1 convolution_convert_fusion.18
  273.8 1.8 copy.112
  275.6 1.6 multiply_reduce_fusion.6
  279.0 2.0 fusion.209
  287.9 1.2 multiply_add_fusion.3
  292.1 2.9 convolution_convert_fusion
  298.8 2.1 convolution_convert_fusion.7
  302.0 2.9 convolution_convert_fusion.1
  306.5 1.1 fusion.44
  308.0 1.7 multiply_reduce_fusion.11
  309.7 2.4 multiply_reduce_fusion.9
  312.9 2.1 convolution_convert_fusion.6
  316.1 3.0 convolution_convert_fusion.5
  323.9 2.1 convolution_convert_fusion.3
  337.5 1.5 convolution_dynamic-update-slice_fusion.15
  339.0 1.5 convolution_dynamic-update-slice_fusion.14
  340.5 1.5 convolution_dynamic-update-slice_fusion.13
  342.0 1.3 convolution_dynamic-update-slice_fusion.12
  343.3 1.5 convolution_dynamic-update-slice_fusion.11
  344.7 1.4 fusion.11
  346.1 1.3 fusion.10
  347.4 1.3 convolution_dynamic-update-slice_fusion.10
  348.7 2.8 convolution_dynamic-update-slice_fusion.3
  351.6 2.8 convolution_dynamic-update-slice_fusion.2
  354.3 12.8 %add.297 = f32[8192,512]{1,0:T(8,128)} add(f32[8192,512]{1,0:T(8,128)} %convolution_dynamic-update-slice_fusion.2, f32[8192,512]{1,0:T(8,128)S(1)} %convolution_dynamic-update-slice_fusion) | non-fusion elementwise | flops 4194304 | bytes 50331648 | tf_op jit(solution)/shard_map/add | solution.py:267
  369.2 1.4 fusion.140
  370.7 1.5 fusion.138
  372.2 1.4 convolution_add_fusion.5
  373.6 1.4 convolution_add_fusion.3
  375.1 1.4 convolution_add_fusion.2
  377.3 2.4 fusion.91
  379.8 550.3 %all-reduce = bf16[6,512]{1,0:T(8,128)(2,1)S(1)} all-reduce(f32[6,512]{1,0:T(8,128)S(1)} %add.303), channel_id=3, replica_groups=mesh['fsdp'=128,'dp'=2] {'fsdp'}, use_global_device_ids=true, to_apply=%region_50.51.clone | all-reduce | flops 3072 | bytes 18432
  930.3 6.4 psum.15
  938.8 1.4 fusion.114
  940.2 1.4 fusion.36
  941.6 1.5 fusion.116
  943.1 1.5 fusion.37
  947.5 2.5 fusion.55
  950.1 2.4 fusion.52
  952.5 4.5 reduce-scatter.3.cloned.1.call-done
  956.9 1.5 convert_element_type.456
  959.3 28.8 %all-reduce.3.cloned.1.call-done = bf16[64,512]{1,0:T(8,128)(2,1)} async-done(((bf16[64,512]{1,0:T(8,128)(2,1)}), bf16[64,512]{1,0:T(8,128)(2,1)}) %all-reduce.3.cloned.1.call-update) | async-done | bytes 65552 | tf_op jit(solution)/shard_map/psum | solution.py:274
  988.2 1.6 multiply_subtract_fusion
  (321 shorter events, 59.2 us)
Async XLA Ops:
  7.2 227.6 %copy-start.6 = (bf16[2,256,512]{2,1,0:T(8,128)(2,1)S(1)}, bf16[2,256,512]{2,1,0:T(8,128)(2,1)}, u32[]{:S(2)}) copy-start(bf16[2,256,512]{2,1,0:T(8,128)(2,1)} %param.9) | copy-start | bytes 1572868
  7.2 226.0 %all-gather.3.cloned.1.call-start = ((), (), s32[]{:S(2)}) async-start(), calls=%async_computation.1 | async-start | bytes 8454144 | tf_op jit(solution)/shard_map/all_gather | solution.py:253
  8.9 948.1 %reduce-scatter.3.cloned.1.call-start = ((), (), s32[]{:S(2)}) async-start(), calls=%async_computation.2 | async-start | bytes 16908288 | tf_op jit(solution)/shard_map/reduce_scatter | solution.py:270
  234.8 32.0 %copy-start.39 = (bf16[256,512]{0,1:T(8,128)(2,1)}, bf16[256,512]{0,1:T(8,128)(2,1)S(1)}, u32[]{:S(2)}) copy-start(bf16[256,512]{0,1:T(8,128)(2,1)S(1)} %copy.108) | copy-start | bytes 786436
  238.7 15.1 %copy-start.35 = (bf16[256,512]{0,1:T(8,128)(2,1)}, bf16[256,512]{0,1:T(8,128)(2,1)S(1)}, u32[]{:S(2)}) copy-start(bf16[256,512]{0,1:T(8,128)(2,1)S(1)} %copy.116) | copy-start | bytes 786436
  240.4 13.4 %copy-start.37 = (bf16[256,512]{0,1:T(8,128)(2,1)}, bf16[256,512]{0,1:T(8,128)(2,1)S(1)}, u32[]{:S(2)}) copy-start(bf16[256,512]{0,1:T(8,128)(2,1)S(1)} %copy.117) | copy-start | bytes 786436
  240.4 4.7 copy-start.66
  261.6 2.0 copy-start.78
  264.5 2.9 copy-start.68
  264.5 2.4 copy-start.41
  269.4 6.2 copy-start.43
  275.6 2.0 copy-start.76
  275.6 5.8 slice-start
  277.6 3.8 slice-start.1
  278.5 2.9 copy-start.70
  278.5 2.9 copy-start.8
  281.0 6.9 copy-start.10
  292.1 3.0 copy-start.3
  292.1 3.0 copy-start.79
  295.7 2.1 copy-start.45
  296.7 2.1 copy-start.16
  301.9 2.9 copy-start.5
  302.0 2.9 copy-start.77
  305.5 2.1 copy-start.44
  307.6 2.0 copy-start.17
  307.6 2.0 copy-start.55
  308.0 4.1 copy-start.85
  316.1 3.0 copy-start.1
  316.1 3.0 copy-start.75
  319.7 2.1 copy-start.42
  320.6 2.2 copy-start.20
  320.7 2.2 copy-start.59
  328.0 3.4 copy-start.33
  334.8 1.6 copy-start.64
  334.8 1.7 copy-start.88
  336.5 2.4 copy-start.51
  337.3 3.1 copy-start.80
  337.5 4.5 copy-start.13
  337.5 4.5 copy-start.94
  340.5 2.8 copy-start.25
  340.5 2.8 copy-start.86
  342.0 2.8 copy-start.50
  343.2 2.8 copy-start.31
  343.3 4.2 copy-start.18
  343.3 4.2 copy-start.71
  346.1 2.6 copy-start.11
  346.1 2.6 copy-start.27
  348.7 2.8 copy-start.61
  367.1 2.1 copy-start.83
  367.1 5.0 copy-start.52
  367.2 621.0 %all-reduce.3.cloned.1.call-start = ((), (), s32[]{:S(2)}) async-start(), calls=%async_computation.3 | async-start | bytes 131072 | tf_op jit(solution)/shard_map/psum | solution.py:274
  369.2 4.4 copy-start.54
  372.2 2.9 copy-start.34
  373.6 3.7 copy-start.81
  377.3 552.9 %copy-start.99 = (f32[6,4]{0,1:T(4,128)S(1)}, f32[6,4]{0,1:T(4,128)}, u32[]{:S(2)}) copy-start(f32[6,4]{0,1:T(4,128)} %param.17) | copy-start | bytes 292
  377.3 561.5 %copy-start.49 = (bf16[8,64,256]{2,1,0:T(8,128)(2,1)S(1)}, bf16[8,64,256]{2,1,0:T(8,128)(2,1)}, u32[]{:S(2)}) copy-start(bf16[8,64,256]{2,1,0:T(8,128)(2,1)} %fusion.45) | copy-start | bytes 786436
  938.8 4.3 copy-start.32
  943.1 2.6 copy-start.58
  943.1 2.6 copy-start.89
  945.7 1.8 copy-start.65
  947.5 2.5 copy-start.62
  950.0 38.2 %copy-start.90 = (f32[64,512]{1,0:T(8,128)S(1)}, f32[64,512]{1,0:T(8,128)}, u32[]{:S(2)}) copy-start(f32[64,512]{1,0:T(8,128)} %param.12) | copy-start | bytes 393220
  950.0 38.2 %copy-start.95 = (f32[64,512]{1,0:T(8,128)S(1)}, f32[64,512]{1,0:T(8,128)}, u32[]{:S(2)}) copy-start(f32[64,512]{1,0:T(8,128)} %param.13) | copy-start | bytes 393220
  950.0 38.1 %copy-start.96 = (f32[64,512]{1,0:T(8,128)S(1)}, f32[64,512]{1,0:T(8,128)}, u32[]{:S(2)}) copy-start(f32[64,512]{1,0:T(8,128)} %param.14) | copy-start | bytes 393220
  (42 other events, 45.5 us)
Sparse Core Ops, SparseCore 0:
  10.5 222.6 all-gather.2
  367.3 589.6 reduce-scatter.2
  960.1 28.0 all-reduce.2
where the time goes:
time: 1010 us; the launch traced here: 997 us
  blocking collectives  716 us (71%)
  matrix products  108 us (11%)
  waiting for transfers between devices  95.1 us (9%)
  local copies, waits for them, and re-layouts  30.9 us (3%)
  other arithmetic  30.1 us (3%)
  between operations  16.4 us (2%)
    unnamed x1, blocking collectives  550 us
    all_gather x1, blocking collectives, local(): lax.all_gather(shards[1], 'fsdp', axis=1, tiled=True)  159 us
    all_gather x1, waiting for transfers between devices, local(): lax.all_gather(shards[0], 'fsdp', axis=0, tiled=True)  61.8 us
    dot_general x20, matrix products, product(): return jnp.dot(former, latter, preferred_element_type=jnp.float32)  31.4 us
    dot_general x20, matrix products, right_product(): lax.dot_general(former, latter, (((1,), (1,)), ((), ())), preferred_eleme...  30.4 us
    psum x1, waiting for transfers between devices, local(): lax.psum(owned_w.astype(jnp.bfloat16), 'dp').astype(jnp.float32)  28.8 us
    dot_general x20, matrix products, left_product(): lax.dot_general(former, latter, (((0,), (0,)), ((), ())), preferred_eleme...  21.7 us
  transfers between devices with their start and end apart: 3, of which 3 were waited for; matrix products, arithmetic and copies ran while one was open for 3% of the time, Pallas kernels for 0%

commit v1 on v0

--- a/solution.py
+++ b/solution.py
@@ -238,26 +238,101 @@
     return (param - rate * (update + DECAY * param), second_new)
 
 
+def exchange(block, axis):
+    return lax.ppermute(block, axis, [(0, 1), (1, 0)])
+
+
+def spread(block, axis, count):
+    return lax.all_to_all(
+        jnp.broadcast_to(block[None], (count,) + block.shape), axis, 0, 0, tiled=True
+    )
+
+
+def in_order(own, other, place):
+    first = jnp.where(place == 0, own, other)
+    second = jnp.where(place == 0, other, own)
+    return first, second
+
+
+def gather_parameters(shard_w, shard_n):
+    along_x, along_core = lax.axis_index("xlo"), lax.axis_index("core")
+    rows, width = shard_w.shape
+    norm_row = jnp.pad(shard_n.reshape(1, -1), ((0, 7), (0, width - shard_n.size)))
+    own = jnp.concatenate([shard_w, norm_row])
+    attn, feed = in_order(own, exchange(own, "xlo"), along_x)
+    norm_row = jnp.concatenate([attn[rows : rows + 1, :24], feed[rows : rows + 1, :24]], axis=1)
+    norm_row = jnp.pad(norm_row, ((0, 7), (0, width - 48)))
+    attn_z = spread(jnp.concatenate([attn[:rows], norm_row]), "z", 8)
+    feed_z = spread(feed[:rows], "z", 8)
+    norm_row = jnp.pad(attn_z[:, rows, :48].reshape(1, -1), ((0, 7), (0, width - 384)))
+    attn_y = spread(jnp.concatenate([attn_z[:, :rows].reshape(8 * rows, width), norm_row]), "y", 4)
+    feed_y = spread(feed_z.reshape(8 * rows, width), "y", 4)
+    attn_c = jnp.stack(in_order(attn_y, exchange(attn_y, "core"), along_core))
+    feed_c = jnp.stack(in_order(feed_y, exchange(feed_y, "core"), along_core))
+    norms = attn_c[:, :, 8 * rows, :384].reshape(2, 4, 8, 2, 6, 4)
+    norms = norms.transpose(4, 3, 2, 1, 0, 5).reshape(6, width)
+
+    def whole(part):
+        return part.reshape(2, 4, 8, rows, width).transpose(2, 1, 0, 3, 4).reshape(64 * rows, width)
+
+    return jnp.concatenate([whole(attn_c[:, :, : 8 * rows]), whole(feed_c)]), norms
+
+
+def pick(block, place):
+    return lax.dynamic_index_in_dim(block, place, 0, keepdims=False)
+
+
+def summed(block, axis, count):
+    moved = lax.all_to_all(block, axis, 0, 0, tiled=True)
+    return moved.reshape((count, -1) + block.shape[1:]).astype(jnp.float32).sum(0)
+
+
+def scatter_gradients(grad_w, grad_n):
+    low = jnp.bfloat16
+    along_x, along_core = lax.axis_index("xlo"), lax.axis_index("core")
+    rows, width = grad_w.shape[0] // 128, grad_w.shape[1]
+    parts = grad_w.reshape(2, 8, 4, 2, rows, width).transpose(3, 0, 2, 1, 4, 5)
+    norms = jnp.pad(grad_n, ((0, 2), (0, 0)))
+    keep = pick(parts, along_core)
+    sent = pick(parts, 1 - along_core).astype(low)
+    keep = keep + exchange(sent, "core").astype(jnp.float32)
+    norms = norms + exchange(norms.astype(low), "core").astype(jnp.float32)
+
+    def with_norms(block, lines):
+        lines = jnp.broadcast_to(lines[None], (block.shape[0], 8, width))
+        return jnp.concatenate([block, lines], axis=1).astype(low)
+
+    sums = []
+    for part in range(2):
+        block = keep[part].reshape(4, 8 * rows, width)
+        if part == 0:
+            block = with_norms(block, norms)
+            block = summed(block, "y", 4)[0]
+            norms = block[8 * rows :]
+            block = with_norms(block[: 8 * rows].reshape(8, rows, width), norms)
+            block = summed(block, "z", 8)[0]
+            norms = block[rows:]
+            sums.append(block[:rows])
+        else:
+            block = summed(block.astype(low), "y", 4)[0]
+            block = summed(block.reshape(8, rows, width).astype(low), "z", 8)[0]
+            sums.append(block)
+    block = with_norms(jnp.stack(sums + sums), norms)
+    block = summed(block, ("xhi", "xlo"), 4)[0]
+    return block[:rows], block[rows : rows + 6]
+
+
 def local(
     inputs, memory, out_grad, weights, first_moment, second_moment, norms, norm_first, norm_second
 ):
-    shards = (weights.astype(jnp.bfloat16), norms.astype(jnp.bfloat16))
-    group_size = lax.axis_size("fsdp")
-    grad_w = jnp.zeros((weights.shape[0] * group_size, weights.shape[1]), jnp.float32)
-    grad_n = jnp.zeros((norms.shape[0], norms.shape[1] * group_size), jnp.float32)
+    full_w, full_n = gather_parameters(weights.astype(jnp.bfloat16), norms.astype(jnp.bfloat16))
+    grad_w = 0.0
+    grad_n = 0.0
     results = []
     grads_start = []
     grads_memory = []
     for sentence in range(inputs.shape[0]):
-        full_w, full_n = (
-            lax.all_gather(shards[0], "fsdp", axis=0, tiled=True),
-            lax.all_gather(shards[1], "fsdp", axis=1, tiled=True),
-        )
         stored, result = forward_pass(inputs[sentence], memory[sentence], full_w, full_n)
-        full_w, full_n = (
-            lax.all_gather(shards[0], "fsdp", axis=0, tiled=True),
-            lax.all_gather(shards[1], "fsdp", axis=1, tiled=True),
-        )
         grad_start, grad_mem, weight_term, norm_term = backward_pass(
             stored, out_grad[sentence], memory[sentence], full_w, full_n
         )
@@ -266,14 +341,9 @@
         grads_memory.append(grad_mem)
         grad_w = grad_w + weight_term
         grad_n = grad_n + norm_term
-    owned_w, owned_n = (
-        lax.psum_scatter(grad_w, "fsdp", scatter_dimension=0, tiled=True),
-        lax.psum_scatter(grad_n, "fsdp", scatter_dimension=1, tiled=True),
-    )
-    owned_w, owned_n = (
-        lax.psum(owned_w.astype(jnp.bfloat16), "dp").astype(jnp.float32),
-        lax.psum(owned_n.astype(jnp.bfloat16), "dp").astype(jnp.float32),
-    )
+    owned_w, all_n = scatter_gradients(grad_w, grad_n)
+    place = lax.axis_index(("xlo", "z", "y", "core"))
+    owned_n = lax.dynamic_slice_in_dim(all_n, place * 4, 4, axis=1)
     new_w, second_w = adam_update(weights, first_moment, second_moment, owned_w, RATE)
     new_n, second_n = adam_update(norms, norm_first, norm_second, owned_n, RATE_NORM)
     outputs = jnp.stack(results).astype(jnp.bfloat16)
@@ -291,30 +361,15 @@
 
 
 def solution(mesh):
+    fsdp = ("xlo", "z", "y", "core")
+    torus = jax.sharding.Mesh(mesh.devices.reshape(2, 8, 4, 2, 2), fsdp + ("xhi",))
+    sentences = P(fsdp + ("xhi",), None, None)
+    rows = P(fsdp, None)
+    columns = P(None, fsdp)
     return jax.shard_map(
         local,
-        mesh=mesh,
-        in_specs=(
-            P(("fsdp", "dp"), None, None),
-            P(("fsdp", "dp"), None, None),
-            P(("fsdp", "dp"), None, None),
-            P("fsdp", None),
-            P("fsdp", None),
-            P("fsdp", None),
-            P(None, "fsdp"),
-            P(None, "fsdp"),
-            P(None, "fsdp"),
-        ),
-        out_specs=(
-            P(("fsdp", "dp"), None, None),
-            P(("fsdp", "dp"), None, None),
-            P(("fsdp", "dp"), None, None),
-            P("fsdp", None),
-            P("fsdp", None),
-            P("fsdp", None),
-            P(None, "fsdp"),
-            P(None, "fsdp"),
-            P(None, "fsdp"),
-        ),
+        mesh=torus,
+        in_specs=(sentences,) * 3 + (rows,) * 3 + (columns,) * 3,
+        out_specs=(sentences,) * 3 + (rows,) * 3 + (columns,) * 3,
         check_vma=False,
     )

time: 1010 us -> 386 us (0.38)
  blocking collectives: 716 us -> 19.4 us
  starting transfers between devices: 0.12 us -> 42.1 us
  waiting for transfers between devices: 95.1 us -> 130 us
  matrix products: 108 us -> 85.7 us
  local copies, waits for them, and re-layouts: 30.9 us -> 51.6 us
  other arithmetic: 30.1 us -> 50.1 us
  between operations: 16.4 us -> 2.73 us
    unnamed x1 -> x0, blocking collectives: 550 us -> none
    all_gather x1 -> x0, blocking collectives: 159 us -> none  [local(): lax.all_gather(shards[1], 'fsdp', axis=1, tiled=True)]
    all_to_all x0 -> x8, waiting for transfers between devices: none -> 123 us  [the longest x5 62.4 us: summed(): moved = lax.all_to_all(block, axis, 0, 0, tiled=True)]
    all_gather x1 -> x0, waiting for transfers between devices: 61.8 us -> none  [local(): lax.all_gather(shards[0], 'fsdp', axis=0, tiled=True)]
    all_to_all x0 -> x8, starting transfers between devices: none -> 38.3 us  [the longest x5 22 us: summed(): moved = lax.all_to_all(block, axis, 0, 0, tiled=True)]
    psum x1 -> x0, waiting for transfers between devices: 28.8 us -> none  [local(): lax.psum(owned_w.astype(jnp.bfloat16), 'dp').astype(jnp.float32)]
    all_to_all x0 -> x1, blocking collectives: none -> 19.4 us  [spread(): lax.all_to_all(jnp.broadcast_to(block[None], (count,) + block.shape), axi...]
    dot_general x20, matrix products: 31.4 us -> 18.7 us  [product(): return jnp.dot(former, latter, preferred_element_type=jnp.float32)]
  transfers between devices with their start and end apart: 3 -> 13, of which waited for: 3 -> 11; matrix products, arithmetic and copies ran while one was open for 3% -> 10% of each run, Pallas kernels for 0% -> 0%
where the time goes in v1:
time: 386 us; the launch traced here: 382 us
  waiting for transfers between devices  130 us (34%)
  matrix products  85.7 us (22%)
  local copies, waits for them, and re-layouts  51.6 us (13%)
  other arithmetic  50.1 us (13%)
  starting transfers between devices  42.1 us (11%)
  blocking collectives  19.4 us (5%)
    all_to_all x5, waiting for transfers between devices, summed(): moved = lax.all_to_all(block, axis, 0, 0, tiled=True)  62.4 us
    all_to_all x3, waiting for transfers between devices, spread(): lax.all_to_all(jnp.broadcast_to(block[None], (count,) + block.shape), axi...  61 us
    dot_general x20, matrix products, right_product(): lax.dot_general(former, latter, (((1,), (1,)), ((), ())), preferred_eleme...  22.1 us
    all_to_all x5, starting transfers between devices, summed(): moved = lax.all_to_all(block, axis, 0, 0, tiled=True)  22 us
    dot_general x20, matrix products, left_product(): lax.dot_general(former, latter, (((0,), (0,)), ((), ())), preferred_eleme...  21.8 us
    unnamed x258, local copies, waits for them, and re-layouts  20.4 us
    all_to_all x1, blocking collectives, spread(): lax.all_to_all(jnp.broadcast_to(block[None], (count,) + block.shape), axi...  19.4 us
    dot_general x20, matrix products, product(): return jnp.dot(former, latter, preferred_element_type=jnp.float32)  18.7 us
  transfers between devices with their start and end apart: 13, of which 11 were waited for; matrix products, arithmetic and copies ran while one was open for 10% of the time, Pallas kernels for 0%

profile of v1, /device:TPU:2, one launch (start us, length us, event | category | flops | bytes accessed | tf_op | source)
XLA Modules:
  0.0 381.8 jit_solution(16121622112031431970)
XLA Ops:
  2.5 2.4 collective-permute-start
  4.8 2.3 collective-permute-done
  8.0 8.2 %all-to-all-start.2 = ((bf16[8,64,512]{2,1,0:T(8,128)(2,1)}), bf16[8,64,512]{2,1,0:T(8,128)(2,1)S(1)}, u32[]{:S(2)}, u32[]{:S(2)}) async-start(bf16[8,64,512]{2,1,0:T(8,128)(2,1)} %broadcast_in_dim.22), calls=%async_computation.2 | async-start | bytes 1048576 | tf_op jit(solution)/shard_map/all_to_all | solution.py:246
  16.4 16.2 %all-to-all-done.2 = bf16[8,64,512]{2,1,0:T(8,128)(2,1)S(1)} async-done(((bf16[8,64,512]{2,1,0:T(8,128)(2,1)}), bf16[8,64,512]{2,1,0:T(8,128)(2,1)S(1)}, u32[]{:S(2)}, u32[]{:S(2)}) %all-to-all-start.2) | async-done | bytes 524320 | tf_op jit(solution)/shard_map/all_to_all | solution.py:246
  32.6 19.4 %all_to_all.45 = bf16[8,72,512]{2,1,0:T(8,128)(2,1)S(1)} all-to-all(bf16[8,72,512]{2,1,0:T(8,128)(2,1)S(1)} %broadcast_in_dim.20), channel_id=1, replica_groups=mesh['xlo'=2,'z'=8,'y'=4,'core'=2,'xhi'=2] {'z'}, dimensions={0} | all-to-all | bytes 1179648 | tf_op jit(solution)/shard_map/all_to_all | solution.py:246
  52.1 1.5 broadcast_in_dim.24
  53.6 4.5 %all-to-all-start.3 = ((bf16[4,512,512]{2,1,0:T(8,128)(2,1)}), bf16[4,512,512]{2,1,0:T(8,128)(2,1)S(1)}, u32[]{:S(2)}, u32[]{:S(2)}) async-start(bf16[4,512,512]{2,1,0:T(8,128)(2,1)} %broadcast_in_dim.24), calls=%async_computation.3 | async-start | bytes 4194304 | tf_op jit(solution)/shard_map/all_to_all | solution.py:246
  58.3 22.6 %all-to-all-done.3 = bf16[4,512,512]{2,1,0:T(8,128)(2,1)S(1)} async-done(((bf16[4,512,512]{2,1,0:T(8,128)(2,1)}), bf16[4,512,512]{2,1,0:T(8,128)(2,1)S(1)}, u32[]{:S(2)}, u32[]{:S(2)}) %all-to-all-start.3) | async-done | bytes 2097184 | tf_op jit(solution)/shard_map/all_to_all | solution.py:246
  80.9 1.6 broadcast_in_dim.21
  82.9 3.6 all-to-all-start.1
  86.6 22.1 %all-to-all-done.1 = bf16[4,520,512]{2,1,0:T(8,128)(2,1)S(1)} async-done(((bf16[4,520,512]{2,1,0:T(8,128)(2,1)}), bf16[4,520,512]{2,1,0:T(8,128)(2,1)S(1)}, u32[]{:S(2)}, u32[]{:S(2)}) %all-to-all-start.1) | async-done | bytes 2129952 | tf_op jit(solution)/shard_map/all_to_all | solution.py:246
  110.2 2.5 broadcast_select_fusion.1
  113.5 1.6 copy.278
  115.1 1.5 copy.279
  116.5 1.9 select_bitcast_fusion.1
  118.9 1.2 fusion.156
  125.5 2.7 fusion.157
  129.7 1.9 convolution_convert_fusion.13
  145.3 1.5 multiply_reduce_fusion.6
  155.3 1.6 multiply_reduce_fusion.4
  162.1 1.8 copy-done.83
  167.9 1.2 multiply_add_fusion.3
  172.0 3.0 convolution_convert_fusion
  180.9 2.9 convolution_convert_fusion.1
  187.7 1.4 multiply_reduce_fusion.9
  210.9 1.5 convolution_dynamic-update-slice_fusion.15
  212.4 1.5 convolution_dynamic-update-slice_fusion.14
  213.9 1.5 convolution_dynamic-update-slice_fusion.13
  215.3 1.3 convolution_dynamic-update-slice_fusion.12
  216.7 1.5 convolution_dynamic-update-slice_fusion.11
  218.1 1.5 fusion.16
  219.7 1.4 fusion.15
  221.0 1.3 convolution_dynamic-update-slice_fusion.10
  222.3 2.8 convolution_dynamic-update-slice_fusion.3
  225.2 2.8 convolution_dynamic-update-slice_fusion.2
  227.9 11.9 %add.324 = f32[8192,512]{1,0:T(8,128)S(1)} add(f32[8192,512]{1,0:T(8,128)} %convolution_dynamic-update-slice_fusion.2, f32[8192,512]{1,0:T(8,128)} %copy-done.11) | non-fusion elementwise | flops 4194304 | bytes 50331648 | tf_op jit(solution)/shard_map/add | solution.py:342
  239.8 5.7 %copy-done.6 = f32[8192,512]{1,0:T(8,128)} copy-done((f32[8192,512]{1,0:T(8,128)}, f32[8192,512]{1,0:T(8,128)S(1)}, u32[]{:S(2)}) %copy-start.6) | copy-done | bytes 16777240
  245.6 2.6 fusion.2
  248.7 1.5 fusion.162
  250.2 2.1 convolution_add_fusion.7
  252.2 3.5 collective-permute-done.3
  255.8 6.2 %fusion.1 = bf16[2,4,8,64,512]{4,3,2,1,0:T(8,128)(2,1)S(1)} fusion(bf16[2,4,8,64,512]{4,3,2,1,0:T(8,128)(2,1)} %collective-permute-done.3, f32[2,8,4,2,64,512]{5,4,3,2,1,0:T(8,128)} %bitcast.405, s32[]{:T(128)S(6)} %select_n.55), kind=kLoop, calls=%fused_computation.3 | loop fusion | flops 6291456 | bytes 16777220 | tf_op jit(solution)/shard_map/convert.17
  262.0 2.3 fusion.154
  264.3 4.4 %all-to-all-start.6 = ((bf16[4,512,512]{2,1,0:T(8,128)(2,1)}), bf16[4,512,512]{2,1,0:T(8,128)(2,1)}, u32[]{:S(2)}, u32[]{:S(2)}) async-start(bf16[4,512,512]{2,1,0:T(8,128)(2,1)} %bitcast.423), calls=%async_computation.6 | async-start | bytes 4194304 | tf_op jit(solution)/shard_map/all_to_all | solution.py:286
  268.8 1.5 fusion.164
  270.4 1.4 convolution_add_fusion.5
  272.2 1.4 fusion.66
  274.9 3.1 pad_maximum_fusion.1
  278.1 17.9 %all-to-all-done.6 = bf16[4,512,512]{2,1,0:T(8,128)(2,1)} async-done(((bf16[4,512,512]{2,1,0:T(8,128)(2,1)}), bf16[4,512,512]{2,1,0:T(8,128)(2,1)}, u32[]{:S(2)}, u32[]{:S(2)}) %all-to-all-start.6) | async-done | bytes 2097184 | tf_op jit(solution)/shard_map/all_to_all | solution.py:286
  296.0 4.4 %all-to-all-start.4 = ((bf16[4,520,512]{2,1,0:T(8,128)(2,1)}), bf16[4,520,512]{2,1,0:T(8,128)(2,1)}, u32[]{:S(2)}, u32[]{:S(2)}) async-start(bf16[4,520,512]{2,1,0:T(8,128)(2,1)} %pad_maximum_fusion.1), calls=%async_computation.4 | async-start | bytes 4259840 | tf_op jit(solution)/shard_map/all_to_all | solution.py:286
  300.5 1.5 fusion.166
  304.7 2.9 reduce_sum.500
  307.6 19.6 %all-to-all-done.4 = bf16[4,520,512]{2,1,0:T(8,128)(2,1)} async-done(((bf16[4,520,512]{2,1,0:T(8,128)(2,1)}), bf16[4,520,512]{2,1,0:T(8,128)(2,1)}, u32[]{:S(2)}, u32[]{:S(2)}) %all-to-all-start.4) | async-done | bytes 2129952 | tf_op jit(solution)/shard_map/all_to_all | solution.py:286
  327.2 4.6 %all-to-all-start.7 = ((bf16[8,64,512]{2,1,0:T(8,128)(2,1)}), bf16[8,64,512]{2,1,0:T(8,128)(2,1)}, u32[]{:S(2)}, u32[]{:S(2)}) async-start(bf16[8,64,512]{2,1,0:T(8,128)(2,1)} %bitcast.492), calls=%async_computation.7 | async-start | bytes 1048576 | tf_op jit(solution)/shard_map/all_to_all | solution.py:286
  331.8 2.3 pad_maximum_fusion.3
  334.1 1.4 fusion.65
  335.5 1.9 convert_reduce_fusion
  338.3 9.9 %all-to-all-done.7 = bf16[8,64,512]{2,1,0:T(8,128)(2,1)} async-done(((bf16[8,64,512]{2,1,0:T(8,128)(2,1)}), bf16[8,64,512]{2,1,0:T(8,128)(2,1)}, u32[]{:S(2)}, u32[]{:S(2)}) %all-to-all-start.7) | async-done | bytes 524320 | tf_op jit(solution)/shard_map/all_to_all | solution.py:286
  348.2 3.5 all-to-all-start.5
  351.8 3.1 fusion.34
  356.0 1.2 reduce.13
  357.2 11.4 %all-to-all-done.5 = bf16[8,72,512]{2,1,0:T(8,128)(2,1)S(1)} async-done(((bf16[8,72,512]{2,1,0:T(8,128)(2,1)}), bf16[8,72,512]{2,1,0:T(8,128)(2,1)S(1)}, u32[]{:S(2)}, u32[]{:S(2)}) %all-to-all-start.5) | async-done | bytes 589856 | tf_op jit(solution)/shard_map/all_to_all | solution.py:286
  369.5 5.0 %all-to-all-start.8 = ((bf16[4,72,512]{2,1,0:T(8,128)(2,1)}), bf16[4,72,512]{2,1,0:T(8,128)(2,1)S(1)}, u32[]{:S(2)}, u32[]{:S(2)}) async-start(bf16[4,72,512]{2,1,0:T(8,128)(2,1)} %pad_maximum_fusion.6), calls=%async_computation.8 | async-start | bytes 589824 | tf_op jit(solution)/shard_map/all_to_all | solution.py:286
  376.4 3.5 all-to-all-done.8
  (444 shorter events, 89.1 us)
Async XLA Ops:
  2.5 4.7 %collective-permute-start = (bf16[72,512]{1,0:T(8,128)(2,1)S(1)}, bf16[72,512]{1,0:T(8,128)(2,1)S(1)}, u32[]{:S(2)}, u32[]{:S(2)}) collective-permute-start(bf16[72,512]{1,0:T(8,128)(2,1)S(1)} %fusion.119), channel_id=1, source_target_pairs={{0,128},{128,0},{1,129},{129,1},{2,130},{130,2},{3,131},{131,3},{4... | collective-permute-start | bytes 221192 | tf_op jit(solution)/shard_map/ppermute | solution.py:242
  8.0 24.6 %all-to-all-start.2 = ((bf16[8,64,512]{2,1,0:T(8,128)(2,1)}), bf16[8,64,512]{2,1,0:T(8,128)(2,1)S(1)}, u32[]{:S(2)}, u32[]{:S(2)}) async-start(bf16[8,64,512]{2,1,0:T(8,128)(2,1)} %broadcast_in_dim.22), calls=%async_computation.2 | async-start | bytes 1048576 | tf_op jit(solution)/shard_map/all_to_all | solution.py:246
  53.6 27.3 %all-to-all-start.3 = ((bf16[4,512,512]{2,1,0:T(8,128)(2,1)}), bf16[4,512,512]{2,1,0:T(8,128)(2,1)S(1)}, u32[]{:S(2)}, u32[]{:S(2)}) async-start(bf16[4,512,512]{2,1,0:T(8,128)(2,1)} %broadcast_in_dim.24), calls=%async_computation.3 | async-start | bytes 4194304 | tf_op jit(solution)/shard_map/all_to_all | solution.py:246
  82.5 26.7 %copy-start.8 = (bf16[2,256,512]{2,1,0:T(8,128)(2,1)S(1)}, bf16[2,256,512]{2,1,0:T(8,128)(2,1)}, u32[]{:S(2)}) copy-start(bf16[2,256,512]{2,1,0:T(8,128)(2,1)} %param.9) | copy-start | bytes 1572868
  82.9 25.9 %all-to-all-start.1 = ((bf16[4,520,512]{2,1,0:T(8,128)(2,1)}), bf16[4,520,512]{2,1,0:T(8,128)(2,1)S(1)}, u32[]{:S(2)}, u32[]{:S(2)}) async-start(bf16[4,520,512]{2,1,0:T(8,128)(2,1)} %broadcast_in_dim.21), calls=%async_computation.1 | async-start | bytes 4259840 | tf_op jit(solution)/shard_map/all_to_all | solution.py:246
  86.5 23.8 %collective-permute-start.2 = (bf16[4,512,512]{2,1,0:T(8,128)(2,1)}, bf16[4,512,512]{2,1,0:T(8,128)(2,1)}, u32[]{:S(2)}, u32[]{:S(2)}) collective-permute-start(bf16[4,512,512]{2,1,0:T(8,128)(2,1)} %copy-done.37), channel_id=1, source_target_pairs={{0,2},{2,0},{1,3},{3,1},{4,6},{6,4},{5,7},{7,5},{8,10},{10,8},{9,1... | collective-permute-start | bytes 6291464 | tf_op jit(solution)/shard_map/ppermute | solution.py:242
  108.7 7.8 %collective-permute-start.1 = (bf16[4,520,512]{2,1,0:T(8,128)(2,1)S(1)}, bf16[4,520,512]{2,1,0:T(8,128)(2,1)}, u32[]{:S(2)}, u32[]{:S(2)}) collective-permute-start(bf16[4,520,512]{2,1,0:T(8,128)(2,1)S(1)} %all-to-all-done.1), channel_id=1, source_target_pairs={{0,2},{2,0},{1,3},{3,1},{4,6},{6,4},{5,7},{7,5},{8,10},{10,8},{9,1... | collective-permute-start | bytes 6389768 | tf_op jit(solution)/shard_map/ppermute | solution.py:242
  129.7 4.1 %copy-start.40 = (bf16[1,4,2,64,512]{4,3,2,1,0:T(8,128)(2,1)}, bf16[1,4,2,64,512]{4,3,2,1,0:T(8,128)(2,1)S(1)}, u32[]{:S(2)}) copy-start(bf16[1,4,2,64,512]{4,3,2,1,0:T(8,128)(2,1)S(1)} %copy.264) | copy-start | bytes 1572868
  129.7 3.0 copy-start.124
  135.7 3.4 copy-start.119
  135.7 3.5 copy-start.118
  136.6 2.8 copy-start.120
  137.3 3.0 copy-start.121
  139.2 10.6 %copy-start.54 = (bf16[256,512]{0,1:T(8,128)(2,1)}, bf16[256,512]{0,1:T(8,128)(2,1)S(1)}, u32[]{:S(2)}) copy-start(bf16[256,512]{0,1:T(8,128)(2,1)S(1)} %copy.282) | copy-start | bytes 786436
  139.4 3.2 copy-start.58
  159.0 8.8 %copy-start.18 = (f32[256,512]{1,0:T(8,128)}, f32[256,512]{1,0:T(8,128)S(1)}, u32[]{:S(2)}) copy-start(f32[256,512]{1,0:T(8,128)S(1)} %get-tuple-element.84) | copy-start | bytes 1572868
  160.7 3.1 copy-start.83
  160.8 3.2 copy-start.109
  161.5 3.5 copy-start.76
  172.0 3.0 copy-start.5
  172.0 3.0 copy-start.117
  180.9 3.0 copy-start.3
  180.9 3.0 copy-start.115
  197.0 3.2 copy-start.1
  201.2 3.7 copy-start.52
  210.8 11.5 %copy-start.11 = (f32[8192,512]{1,0:T(8,128)}, f32[8192,512]{1,0:T(8,128)S(1)}, u32[]{:S(2)}) copy-start(f32[8192,512]{1,0:T(8,128)S(1)} %convolution_dynamic-update-slice_fusion) | copy-start | bytes 50331652
  210.8 3.1 copy-start.103
  210.9 4.4 %copy-start.25 = (f32[256,512]{1,0:T(8,128)S(1)}, f32[256,512]{1,0:T(8,128)}, u32[]{:S(2)}) copy-start(f32[256,512]{1,0:T(8,128)} %copy-done.24) | copy-start | bytes 1572868
  210.9 4.4 %copy-start.98 = (bf16[8,64,256]{2,1,0:T(8,128)(2,1)S(1)}, bf16[8,64,256]{2,1,0:T(8,128)(2,1)}, u32[]{:S(2)}) copy-start(bf16[8,64,256]{2,1,0:T(8,128)(2,1)} %copy-done.97) | copy-start | bytes 786436
  213.9 2.8 copy-start.108
  215.3 2.8 copy-start.67
  216.7 3.0 copy-start.50
  216.7 4.4 %copy-start.33 = (f32[256,512]{1,0:T(8,128)S(1)}, f32[256,512]{1,0:T(8,128)}, u32[]{:S(2)}) copy-start(f32[256,512]{1,0:T(8,128)} %get-tuple-element.62) | copy-start | bytes 1572868
  216.7 4.4 %copy-start.90 = (bf16[8,64,256]{2,1,0:T(8,128)(2,1)S(1)}, bf16[8,64,256]{2,1,0:T(8,128)(2,1)}, u32[]{:S(2)}) copy-start(bf16[8,64,256]{2,1,0:T(8,128)(2,1)} %copy-done.89) | copy-start | bytes 786436
  219.7 2.7 copy-start.17
  219.7 2.7 copy-start.46
  222.3 2.8 copy-start.80
  239.8 5.7 %copy-start.6 = (f32[8192,512]{1,0:T(8,128)}, f32[8192,512]{1,0:T(8,128)S(1)}, u32[]{:S(2)}) copy-start(f32[8192,512]{1,0:T(8,128)S(1)} %add.324) | copy-start | bytes 50331652
  245.6 4.6 %copy-start.41 = (bf16[1,4,2,64,512]{4,3,2,1,0:T(8,128)(2,1)S(1)}, bf16[1,4,2,64,512]{4,3,2,1,0:T(8,128)(2,1)}, u32[]{:S(2)}) copy-start(bf16[1,4,2,64,512]{4,3,2,1,0:T(8,128)(2,1)} %copy-done.40) | copy-start | bytes 1572868
  248.2 7.6 %collective-permute-start.3 = (bf16[2,4,8,64,512]{4,3,2,1,0:T(8,128)(2,1)}, bf16[2,4,8,64,512]{4,3,2,1,0:T(8,128)(2,1)}, u32[]{:S(2)}, u32[]{:S(2)}) collective-permute-start(bf16[2,4,8,64,512]{4,3,2,1,0:T(8,128)(2,1)} %fusion.2), channel_id=1, source_target_pairs={{0,2},{2,0},{1,3},{3,1},{4,6},{6,4},{5,7},{7,5},{8,10},{10,8},{9,1... | collective-permute-start | bytes 12582920 | tf_op jit(solution)/shard_map/ppermute | solution.py:242
  264.3 31.7 %all-to-all-start.6 = ((bf16[4,512,512]{2,1,0:T(8,128)(2,1)}), bf16[4,512,512]{2,1,0:T(8,128)(2,1)}, u32[]{:S(2)}, u32[]{:S(2)}) async-start(bf16[4,512,512]{2,1,0:T(8,128)(2,1)} %bitcast.423), calls=%async_computation.6 | async-start | bytes 4194304 | tf_op jit(solution)/shard_map/all_to_all | solution.py:286
  268.8 3.0 copy-start.53
  268.8 3.0 copy-start.82
  272.1 2.8 copy-start.73
  273.6 1.3 collective-permute-start.4
  278.1 24.0 %copy-start.39 = (bf16[1,4,2,64,512]{4,3,2,1,0:T(8,128)(2,1)S(1)}, bf16[1,4,2,64,512]{4,3,2,1,0:T(8,128)(2,1)}, u32[]{:S(2)}) copy-start(bf16[1,4,2,64,512]{4,3,2,1,0:T(8,128)(2,1)} %copy-done.38) | copy-start | bytes 1572868
  296.0 31.2 %all-to-all-start.4 = ((bf16[4,520,512]{2,1,0:T(8,128)(2,1)}), bf16[4,520,512]{2,1,0:T(8,128)(2,1)}, u32[]{:S(2)}, u32[]{:S(2)}) async-start(bf16[4,520,512]{2,1,0:T(8,128)(2,1)} %pad_maximum_fusion.1), calls=%async_computation.4 | async-start | bytes 4259840 | tf_op jit(solution)/shard_map/all_to_all | solution.py:286
  300.4 2.8 copy-start.43
  300.5 2.7 copy-start.68
  300.5 3.1 copy-start.51
  307.6 26.5 %copy-start.74 = (f32[256,512]{1,0:T(8,128)S(1)}, f32[256,512]{1,0:T(8,128)}, u32[]{:S(2)}) copy-start(f32[256,512]{1,0:T(8,128)} %copy-done.73) | copy-start | bytes 1572868
  327.2 21.0 %all-to-all-start.7 = ((bf16[8,64,512]{2,1,0:T(8,128)(2,1)}), bf16[8,64,512]{2,1,0:T(8,128)(2,1)}, u32[]{:S(2)}, u32[]{:S(2)}) async-start(bf16[8,64,512]{2,1,0:T(8,128)(2,1)} %bitcast.492), calls=%async_computation.7 | async-start | bytes 1048576 | tf_op jit(solution)/shard_map/all_to_all | solution.py:286
  348.2 20.5 %all-to-all-start.5 = ((bf16[8,72,512]{2,1,0:T(8,128)(2,1)}), bf16[8,72,512]{2,1,0:T(8,128)(2,1)S(1)}, u32[]{:S(2)}, u32[]{:S(2)}) async-start(bf16[8,72,512]{2,1,0:T(8,128)(2,1)} %pad_maximum_fusion.4), calls=%async_computation.5 | async-start | bytes 1179648 | tf_op jit(solution)/shard_map/all_to_all | solution.py:286
  351.8 3.1 copy-start.78
  351.8 3.5 copy-start.84
  356.0 19.3 %copy-start.85 = (f32[1,256,512]{2,1,0:T(8,128)S(1)}, f32[1,256,512]{2,1,0:T(8,128)}, u32[]{:S(2)}) copy-start(f32[1,256,512]{2,1,0:T(8,128)} %get-tuple-element.60) | copy-start | bytes 1572868
  356.0 19.3 %copy-start.86 = (f32[1,256,512]{2,1,0:T(8,128)S(1)}, f32[1,256,512]{2,1,0:T(8,128)}, u32[]{:S(2)}) copy-start(f32[1,256,512]{2,1,0:T(8,128)} %get-tuple-element.61) | copy-start | bytes 1572868
  369.5 10.6 %copy-start.113 = (f32[64,512]{1,0:T(8,128)S(1)}, f32[64,512]{1,0:T(8,128)}, u32[]{:S(2)}) copy-start(f32[64,512]{1,0:T(8,128)} %param.12) | copy-start | bytes 393220
  369.5 10.6 %copy-start.122 = (f32[64,512]{1,0:T(8,128)S(1)}, f32[64,512]{1,0:T(8,128)}, u32[]{:S(2)}) copy-start(f32[64,512]{1,0:T(8,128)} %param.13) | copy-start | bytes 393220
  369.5 10.6 %copy-start.123 = (f32[64,512]{1,0:T(8,128)S(1)}, f32[64,512]{1,0:T(8,128)}, u32[]{:S(2)}) copy-start(f32[64,512]{1,0:T(8,128)} %param.14) | copy-start | bytes 393220
  369.5 10.4 %all-to-all-start.8 = ((bf16[4,72,512]{2,1,0:T(8,128)(2,1)}), bf16[4,72,512]{2,1,0:T(8,128)(2,1)S(1)}, u32[]{:S(2)}, u32[]{:S(2)}) async-start(bf16[4,72,512]{2,1,0:T(8,128)(2,1)} %pad_maximum_fusion.6), calls=%async_computation.8 | async-start | bytes 589824 | tf_op jit(solution)/shard_map/all_to_all | solution.py:286
  374.5 6.5 %copy-start.126 = (f32[6,4]{0,1:T(4,128)S(1)}, f32[6,4]{0,1:T(4,128)}, u32[]{:S(2)}) copy-start(f32[6,4]{0,1:T(4,128)} %param.15) | copy-start | bytes 292
  374.5 6.5 %copy-start.127 = (f32[6,4]{0,1:T(4,128)S(1)}, f32[6,4]{0,1:T(4,128)}, u32[]{:S(2)}) copy-start(f32[6,4]{0,1:T(4,128)} %param.16) | copy-start | bytes 292
  374.5 6.5 %copy-start.128 = (f32[6,4]{0,1:T(4,128)S(1)}, f32[6,4]{0,1:T(4,128)}, u32[]{:S(2)}) copy-start(f32[6,4]{0,1:T(4,128)} %param.17) | copy-start | bytes 292
  (78 other events, 118.1 us)

commit v2 on v0

v2 whole, which is shorter than its diff:
```python
import jax
import jax.numpy as jnp
from jax import lax
from jax.experimental import pallas as pl
from jax.experimental.pallas import tpu as pltpu
from jax.sharding import PartitionSpec as P

LOW = jnp.bfloat16
WIDE = jnp.float32
HEADS = 8
HEAD = 64
LEN = 256
D = 512
FF = 2048
TOK = 512
EPS_NORM = 1e-05


def dot(former, latter, left, right):
    return lax.dot_general(
        former, latter, (((left,), (right,)), ((), ())), preferred_element_type=WIDE
    )


def nn(former, latter):
    return dot(former, latter, 1, 0)


def nt(former, latter):
    return dot(former, latter, 1, 1)


def tn(former, latter):
    return dot(former, latter, 0, 0)


def normalise(vector):
    centre = vector - jnp.mean(vector, axis=-1, keepdims=True)
    factor = lax.rsqrt(jnp.mean(centre * centre, axis=-1, keepdims=True) + EPS_NORM)
    return centre * factor, factor


def norm_back(grad, normed, factor, gain):
    scaled = grad * gain
    mean_one = jnp.mean(scaled, axis=-1, keepdims=True)
    mean_two = jnp.mean(scaled * normed, axis=-1, keepdims=True)
    return (
        factor * (scaled - mean_one - normed * mean_two),
        jnp.sum(grad * normed, axis=0, keepdims=True),
        jnp.sum(grad, axis=0, keepdims=True),
    )


def half_mask(which):
    lane = lax.broadcasted_iota(jnp.int32, (LEN, 128), 1)
    return (lane >= 64) if which else (lane < 64)


def attend(q_ref, k_ref, v_ref, prob_ref, mixed_ref):
    masks = [half_mask(0), half_mask(1)]
    zero = jnp.zeros((LEN, 128), LOW)
    for s in range(2):
        rows = pl.ds(s * LEN, LEN)
        for pair in range(4):
            cols = pl.ds(pair * 128, 128)
            queries, keys = q_ref[rows, cols], k_ref[rows, cols]
            values = v_ref[rows, cols].T
            for j in range(2):
                scores = nt(jnp.where(masks[j], keys, zero), queries)
                top = jnp.max(scores, axis=0, keepdims=True)
                raised = jnp.exp(scores - top)
                total = jnp.sum(raised, axis=0, keepdims=True)
                soft = (raised * (1.0 / total)).astype(LOW)
                prob_ref[s * 8 + pair * 2 + j] = soft
                mixed = nn(values[j * 64 : (j + 1) * 64], soft)
                mixed_ref[s, pl.ds(pair * 128 + j * 64, 64)] = mixed.astype(LOW)


def attend_back(q_ref, k_ref, v_ref, prob_ref, go_ref, dq_ref, dk_ref, dv_ref):
    masks = [half_mask(0), half_mask(1)]
    zero = jnp.zeros((LEN, 128), LOW)
    for s in range(2):
        rows = pl.ds(s * LEN, LEN)
        for pair in range(4):
            cols = pl.ds(pair * 128, 128)
            queries, keys, values = q_ref[rows, cols], k_ref[rows, cols], v_ref[rows, cols]
            grad_out = go_ref[rows, cols]
            keys_t = keys.T
            parts_q, parts_k, parts_v = [], [], []
            for j in range(2):
                soft = prob_ref[s * 8 + pair * 2 + j]
                grad_soft = nt(jnp.where(masks[j], values, zero), grad_out)
                wide = soft.astype(WIDE)
                weighed = wide * grad_soft
                inner = jnp.sum(weighed, axis=0, keepdims=True)
                grad_scores = (weighed - wide * inner).astype(LOW)
                parts_v.append(nn(soft, grad_out))
                parts_k.append(nn(grad_scores, queries))
                parts_q.append(nn(keys_t[j * 64 : (j + 1) * 64], grad_scores))
            dv_ref[rows, cols] = jnp.where(masks[0], parts_v[0], parts_v[1]).astype(LOW)
            dk_ref[rows, cols] = jnp.where(masks[0], parts_k[0], parts_k[1]).astype(LOW)
            grad_q = jnp.concatenate(parts_q, axis=0) * HEAD ** (-0.5)
            dq_ref[rows, cols] = grad_q.astype(LOW).T


def weight_copies(core, own, oth, held, sem, first, count):
    copies = []
    for place, source in ((core, own), (1 - core, oth)):
        for y in range(4):
            for b in range(count):
                copies.append(
                    pltpu.make_async_copy(
                        source.at[y, pl.ds((first + b) * 64, 64)], held.at[b, y, place], sem
                    )
                )
    for copy in copies:
        copy.start()
    return copies


def wait_all(copies):
    for copy in copies:
        copy.wait()


def block(held, b):
    return held[b].reshape(D, D)


def self_forward(core_ref, x_ref, own, oth, q, k, v, prob, mixed, after, norms, held, pieces, sem):
    core = core_ref[0]
    copies = []
    for place, source in ((0, own), (1, oth)):
        for y in range(4):
            copies.append(
                pltpu.make_async_copy(
                    source.at[y, pl.ds(512, 16)], pieces.at[place * 4 + y], sem.at[0]
                )
            )
    for copy in copies:
        copy.start()
    weights = weight_copies(core, own, oth, held, sem.at[1], 0, 4)
    start = x_ref[...].astype(WIDE)
    normed, _ = normalise(start)
    wait_all(copies)
    rows = jnp.sum(pieces[...].astype(WIDE), axis=0)
    norms[...] = rows[:8]
    first_in = (normed * rows[0:1] + rows[1:2]).astype(LOW)
    wait_all(weights)
    q[...] = nn(first_in, block(held, 0)).astype(LOW) * LOW(HEAD ** (-0.5))
    k[...] = nn(first_in, block(held, 1)).astype(LOW)
    v[...] = nn(first_in, block(held, 2)).astype(LOW)
    attend(q, k, v, prob, mixed)
    for s in range(2):
        lines = pl.ds(s * LEN, LEN)
        after[lines, :] = x_ref[lines, :].astype(WIDE) + tn(mixed[s], block(held, 3))


def cross_forward(core_ref, x_ref, m_ref, n_ref, own, oth, q, k, v, prob, mixed, after, held, sem):
    core = core_ref[0]
    weights = weight_copies(core, own, oth, held, sem.at[0], 4, 4)
    normed, _ = normalise(x_ref[...])
    second_in = (normed * n_ref[2:3] + n_ref[3:4]).astype(LOW)
    wait_all(weights)
    q[...] = nn(second_in, block(held, 0)).astype(LOW) * LOW(HEAD ** (-0.5))
    k[...] = nn(m_ref[...], block(held, 1)).astype(LOW)
    v[...] = nn(m_ref[...], block(held, 2)).astype(LOW)
    attend(q, k, v, prob, mixed)
    for s in range(2):
        lines = pl.ds(s * LEN, LEN)
        after[lines, :] = x_ref[lines, :] + tn(mixed[s], block(held, 3))


def store_grad(grads, place, core, b, value):
    parts = value.astype(LOW).reshape(4, 2, 64, D)
    for c in range(2):
        grads[lax.rem(core + c, 2), :, b] = parts[:, c]


def feed_both(core_ref, x_ref, g_ref, n_ref, own, oth, result, back, kept, sent, rows_out,
              held_in, held_down, grads, sem):
    core = core_ref[0]
    weights = [
        (
            weight_copies(core, own, oth, held_in.at[pl.ds(c, 1)], sem.at[c], c, 1),
            weight_copies(core, own, oth, held_down.at[pl.ds(c, 1)], sem.at[c + 4], 4 + c, 1),
        )
        for c in range(4)
    ]
    start = x_ref[...]
    normed, factor = normalise(start)
    third_in = (normed * n_ref[4:5] + n_ref[5:6]).astype(LOW)
    grad_low = g_ref[...]
    forward = start
    grad_in = jnp.zeros((TOK, D), WIDE)
    for c in range(4):
        wait_all(weights[c][0])
        w_in = block(held_in, c)
        up = nt(third_in, w_in)
        wait_all(weights[c][1])
        w_down = block(held_down, c)
        grad_act = nt(grad_low, w_down)
        sigma = 1.0 / (1.0 + jnp.exp(-up))
        active = up * sigma
        grad_up = (grad_act * (sigma + active * (1.0 - sigma))).astype(LOW)
        active = active.astype(LOW)
        forward = forward + nn(active, w_down)
        grad_in = grad_in + nn(grad_up, w_in)
        store_grad(grads, 0, core, c, tn(grad_up, third_in))
        store_grad(grads, 0, core, 4 + c, tn(active, grad_low))
    result[...] = forward.astype(LOW)
    first = pltpu.make_async_copy(grads.at[0], kept, sem.at[8])
    second = pltpu.make_async_copy(grads.at[1], sent, sem.at[9])
    second.start()
    first.start()
    grad, gain, bias = norm_back(grad_in, normed, factor, n_ref[4:5])
    back[...] = grad_low.astype(WIDE) + grad
    rows_out[...] = jnp.concatenate([gain, bias, jnp.zeros((6, D), WIDE)])
    second.wait()
    first.wait()


def cross_back(core_ref, d_ref, x_ref, m_ref, n_ref, own, oth, q, k, v, prob, mixed, back, dk, dv,
               kept, sent, rows_out, held, go, dq, grads, sem):
    core = core_ref[0]
    weights = weight_copies(core, own, oth, held, sem.at[0], 4, 4)
    down = d_ref[...].astype(LOW)
    wait_all(weights)
    go[...] = nt(down, block(held, 3)).astype(LOW)
    total = nn(mixed[0], down[:LEN]) + nn(mixed[1], down[LEN:])
    store_grad(grads, 0, core, 3, total)
    attend_back(q, k, v, prob, go, dq, dk, dv)
    normed, factor = normalise(x_ref[...])
    second_in = (normed * n_ref[2:3] + n_ref[3:4]).astype(LOW)
    grad_in = nt(dq[...], block(held, 0))
    store_grad(grads, 0, core, 0, tn(second_in, dq[...]))
    memory = m_ref[...]
    store_grad(grads, 0, core, 1, tn(memory, dk[...]))
    store_grad(grads, 0, core, 2, tn(memory, dv[...]))
    first = pltpu.make_async_copy(grads.at[0], kept, sem.at[1])
    second = pltpu.make_async_copy(grads.at[1], sent, sem.at[2])
    second.start()
    first.start()
    grad, gain, bias = norm_back(grad_in, normed, factor, n_ref[2:3])
    back[...] = d_ref[...] + grad
    rows_out[...] = jnp.concatenate([gain, bias, jnp.zeros((6, D), WIDE)])
    second.wait()
    first.wait()


def self_back(core_ref, d_ref, x_ref, n_ref, own, oth, q, k, v, prob, mixed, dq, dk, dv,
              kept, sent, held, go, grads, sem):
    core = core_ref[0]
    weights = weight_copies(core, own, oth, held, sem.at[0], 3, 1)
    down = d_ref[...].astype(LOW)
    wait_all(weights)
    go[...] = nt(down, block(held, 0)).astype(LOW)
    total = nn(mixed[0], down[:LEN]) + nn(mixed[1], down[LEN:])
    store_grad(grads, 0, core, 3, total)
    attend_back(q, k, v, prob, go, dq, dk, dv)
    normed, factor = normalise(x_ref[...].astype(WIDE))
    first_in = (normed * n_ref[0:1] + n_ref[1:2]).astype(LOW)
    store_grad(grads, 0, core, 0, tn(first_in, dq[...]))
    store_grad(grads, 0, core, 1, tn(first_in, dk[...]))
    store_grad(grads, 0, core, 2, tn(first_in, dv[...]))
    first = pltpu.make_async_copy(grads.at[0], kept, sem.at[1])
    second = pltpu.make_async_copy(grads.at[1], sent, sem.at[2])
    second.start()
    first.start()
    second.wait()
    first.wait()


def last_back(core_ref, d_ref, x_ref, n_ref, own, oth, dq, dk, dv, dkc, dvc, back, back_m, rows_out,
              held, sem):
    core = core_ref[0]
    weights = weight_copies(core, own, oth, held, sem.at[0], 0, 3)
    cross = weight_copies(core, own, oth, held.at[pl.ds(3, 2)], sem.at[1], 5, 2)
    normed, factor = normalise(x_ref[...].astype(WIDE))
    wait_all(weights)
    grad_in = nt(dq[...], block(held, 0)) + nt(dk[...], block(held, 1)) + nt(dv[...], block(held, 2))
    grad, gain, bias = norm_back(grad_in, normed, factor, n_ref[0:1])
    back[...] = d_ref[...] + grad
    rows_out[...] = jnp.concatenate([gain, bias, jnp.zeros((6, D), WIDE)])
    wait_all(cross)
    back_m[...] = nt(dkc[...], block(held, 3)) + nt(dvc[...], block(held, 4))


SMALL = pl.BlockSpec(memory_space=pltpu.SMEM)
NEAR = pl.BlockSpec(memory_space=pltpu.VMEM)
FAR = pl.BlockSpec(memory_space=pl.ANY)
DMA = pltpu.SemaphoreType.DMA


def shape(*dims, dtype=LOW):
    return jax.ShapeDtypeStruct(dims, dtype)


def call(kernel, ins, outs, scratch, flops, name):
    return pl.pallas_call(
        kernel,
        in_specs=ins,
        out_specs=[spec for spec, _ in outs],
        out_shape=[form for _, form in outs],
        scratch_shapes=scratch,
        name=name,
        compiler_params=pltpu.CompilerParams(vmem_limit_bytes=56 * 2**20),
        cost_estimate=pl.CostEstimate(flops=flops, bytes_accessed=8 * 2**20, transcendentals=0),
    )


TOKENS = (NEAR, shape(TOK, D))
TOKENS_WIDE = (NEAR, shape(TOK, D, dtype=WIDE))
PROBS = (NEAR, shape(16, LEN, LEN))
MIXED = (NEAR, shape(2, D, LEN))
LINES = (NEAR, shape(8, D, dtype=WIDE))
HALF = (FAR, shape(4, 4, 64, D))
FULL = (FAR, shape(4, 8, 64, D))


def held(count):
    return pltpu.VMEM((count, 4, 2, 64, D), LOW)


def grads(count):
    return pltpu.VMEM((2, 4, count, 64, D), LOW)


run_self_forward = call(
    self_forward, [SMALL, NEAR, FAR, FAR],
    [TOKENS, TOKENS, TOKENS, PROBS, MIXED, TOKENS_WIDE, LINES],
    [held(4), pltpu.VMEM((8, 16, D), LOW), DMA((2,))], 2 * 7 * 10**8, "self_forward")
run_cross_forward = call(
    cross_forward, [SMALL, NEAR, NEAR, NEAR, FAR, FAR],
    [TOKENS, TOKENS, TOKENS, PROBS, MIXED, TOKENS_WIDE],
    [held(4), DMA((1,))], 2 * 7 * 10**8, "cross_forward")
run_feed_both = call(
    feed_both, [SMALL, NEAR, NEAR, NEAR, FAR, FAR],
    [TOKENS, TOKENS_WIDE, FULL, FULL, LINES],
    [held(4), held(4), grads(8), DMA((10,))], 2 * 33 * 10**8, "feed_both")
run_cross_back = call(
    cross_back, [SMALL, NEAR, NEAR, NEAR, NEAR, FAR, FAR] + [NEAR] * 5,
    [TOKENS_WIDE, TOKENS, TOKENS, HALF, HALF, LINES],
    [held(4), pltpu.VMEM((TOK, D), LOW), pltpu.VMEM((TOK, D), LOW), grads(4), DMA((3,))],
    2 * 12 * 10**8, "cross_back")
run_self_back = call(
    self_back, [SMALL, NEAR, NEAR, NEAR, FAR, FAR] + [NEAR] * 5,
    [TOKENS, TOKENS, TOKENS, HALF, HALF],
    [held(1), pltpu.VMEM((TOK, D), LOW), grads(4), DMA((3,))], 2 * 12 * 10**8, "self_back")
run_last_back = call(
    last_back, [SMALL, NEAR, NEAR, NEAR, FAR, FAR] + [NEAR] * 5,
    [TOKENS_WIDE, TOKENS_WIDE, LINES],
    [held(5), DMA((2,))], 2 * 7 * 10**8, "last_back")


STEP = 10
BETA_ONE = 0.9
BETA_TWO = 0.98
RATE = 0.1
RATE_NORM = 0.4
DECAY = 0.01
EPS_ADAM = 1e-09
SHARD = 64
FSDP = ("xlo", "z", "y", "core")


def exchange(part, axis):
    return lax.ppermute(part, axis, [(0, 1), (1, 0)])


def spread(part, axis, count):
    return lax.all_to_all(
        jnp.broadcast_to(part[None], (count,) + part.shape), axis, 0, 0, tiled=True
    )


def summed(part, axis):
    return lax.all_to_all(part, axis, 0, 0, tiled=True).astype(WIDE).sum(0)


def both(own, other):
    return (own.astype(WIDE) + other.astype(WIDE)).astype(LOW)


def gather_parameters(shard_w, shard_n):
    along_x = lax.axis_index("xlo")
    place = lax.axis_index(FSDP)
    lines = lax.dynamic_update_slice(jnp.zeros((16, D), LOW), shard_n, (0, place * 4))
    own = jnp.concatenate([shard_w, lines])
    other = exchange(own, "xlo")
    lines = own[SHARD:] + other[SHARD:]
    attn = jnp.where(along_x == 0, own[:SHARD], other[:SHARD])
    feed = jnp.where(along_x == 0, other[:SHARD], own[:SHARD])
    attn_z = spread(jnp.concatenate([attn, lines]), "z", 8)
    attn_z, feed = lax.optimization_barrier((attn_z, feed))
    feed_z = spread(feed, "z", 8)
    lines = attn_z[:, SHARD:].sum(0)
    attn_y = spread(jnp.concatenate([attn_z[:, :SHARD].reshape(8 * SHARD, D), lines]), "y", 4)
    attn_c = exchange(attn_y, "core")
    feed_y = spread(feed_z.reshape(8 * SHARD, D), "y", 4)
    feed_c = exchange(feed_y, "core")
    return attn_y, attn_c, feed_y, feed_c


def adam_update(param, first, second, grad, rate):
    first_new = BETA_ONE * first + (1.0 - BETA_ONE) * grad
    second_new = BETA_TWO * second + (1.0 - BETA_TWO) * grad * grad
    fix_one = 1.0 - BETA_ONE**STEP
    fix_two = 1.0 - BETA_TWO**STEP
    update = first_new / fix_one / (jnp.sqrt(second_new / fix_two) + EPS_ADAM)
    return (param - rate * (update + DECAY * param), second_new)


def local(
    inputs, memory, out_grad, weights, first_moment, second_moment, norms, norm_first, norm_second
):
    core = lax.axis_index("core").astype(jnp.int32).reshape(1)
    x, m, g = (part.reshape(TOK, D) for part in (inputs, memory, out_grad))
    own_a, oth_a, own_f, oth_f = gather_parameters(weights.astype(LOW), norms.astype(LOW))
    *kept_one, after_one, rows = run_self_forward(core, x, own_a, oth_a)
    *kept_two, after_two = run_cross_forward(core, after_one, m, rows, own_a, oth_a)
    result, grad_two, keep, sent, lines_three = run_feed_both(
        core, after_two, g, rows, own_f, oth_f
    )
    feed = both(keep, exchange(sent, "core"))
    grad_one, grad_kc, grad_vc, keep, sent, lines_two = run_cross_back(
        core, grad_two, after_one, m, rows, own_a, oth_a, *kept_two
    )
    cross = both(keep, exchange(sent, "core"))
    feed = summed(feed, "y")
    grad_q, grad_k, grad_v, keep, sent = run_self_back(
        core, grad_one, x, rows, own_a, oth_a, *kept_one
    )
    own = both(keep, exchange(sent, "core"))
    cross = summed(cross, "y")
    feed = summed(feed.astype(LOW), "z")
    grad_start, grad_memory, lines_one = run_last_back(
        core, grad_one, x, rows, own_a, oth_a, grad_q, grad_k, grad_v, grad_kc, grad_vc
    )
    lines = jnp.concatenate(
        [lines_one[:2], lines_two[:2], lines_three[:2], jnp.zeros((10, D), WIDE)]
    ).astype(LOW)
    lines = both(lines, exchange(lines, "core"))
    own = summed(own, "y")
    lines = lax.all_to_all(
        jnp.broadcast_to(lines[None], (4, 16, D)), "y", 0, 0, tiled=True
    ).astype(WIDE).sum(0).astype(LOW)
    attn = jnp.concatenate([own, cross], axis=0).astype(LOW)
    attn = jnp.concatenate([attn, jnp.broadcast_to(lines[None], (8, 16, D))], axis=1)
    attn = summed(attn, "z").astype(LOW)
    feed = jnp.concatenate([feed.astype(LOW), attn[SHARD:]])
    last = summed(jnp.stack([attn, feed, attn, feed]), ("xhi", "xlo"))
    owned_w = last[:SHARD]
    place = lax.axis_index(FSDP)
    owned_n = lax.dynamic_slice(last[SHARD : SHARD + 6], (0, place * 4), (6, 4))
    new_w, second_w = adam_update(weights, first_moment, second_moment, owned_w, RATE)
    new_n, second_n = adam_update(norms, norm_first, norm_second, owned_n, RATE_NORM)
    return (
        result.reshape(inputs.shape),
        grad_start.reshape(inputs.shape),
        grad_memory.reshape(inputs.shape),
        owned_w,
        new_w,
        second_w,
        owned_n,
        new_n,
        second_n,
    )


def solution(mesh):
    torus = jax.sharding.Mesh(mesh.devices.reshape(2, 8, 4, 2, 2), FSDP + ("xhi",))
    sentences = P(FSDP + ("xhi",), None, None)
    rows = P(FSDP, None)
    columns = P(None, FSDP)
    return jax.shard_map(
        local,
        mesh=torus,
        in_specs=(sentences,) * 3 + (rows,) * 3 + (columns,) * 3,
        out_specs=(sentences,) * 3 + (rows,) * 3 + (columns,) * 3,
        check_vma=False,
    )
```

time: 1010 us -> 318 us (0.31)
  blocking collectives: 716 us -> 55.4 us
  matrix products: 108 us -> 0 us
  Pallas kernels: 0 us -> 69.9 us
  starting transfers between devices: 0.12 us -> 38.4 us
  waiting for transfers between devices: 95.1 us -> 119 us
  local copies, waits for them, and re-layouts: 30.9 us -> 13.1 us
  between operations: 16.4 us -> 1.49 us
  other arithmetic: 30.1 us -> 16 us
    unnamed x1 -> x0, blocking collectives: 550 us -> none
    all_gather x1 -> x0, blocking collectives: 159 us -> none  [local(): lax.all_gather(shards[1], 'fsdp', axis=1, tiled=True)]
    all_to_all x0 -> x9, waiting for transfers between devices: none -> 115 us  [the longest x6 76.8 us: summed(): return lax.all_to_all(part, axis, 0, 0, tiled=True).astype(WIDE).sum(0)]
    dot_general x84 -> x0, matrix products: 108 us -> none  [the longest x20 31.4 us: product(): return jnp.dot(former, latter, preferred_element_type=jnp.float32)]
    pallas_call x0 -> x6, Pallas kernels: none -> 69.9 us  [the longest x1 14.8 us: local(): run_feed_both(core, after_two, g, rows, own_f, oth_f)]
    all_gather x1 -> x0, waiting for transfers between devices: 61.8 us -> none  [local(): lax.all_gather(shards[0], 'fsdp', axis=0, tiled=True)]
    all_to_all x0 -> x2, blocking collectives: none -> 55.4 us  [spread(): lax.all_to_all(jnp.broadcast_to(part[None], (count,) + part.shape), axis,...]
    all_to_all x0 -> x9, starting transfers between devices: none -> 34.5 us  [the longest x6 23.3 us: summed(): return lax.all_to_all(part, axis, 0, 0, tiled=True).astype(WIDE).sum(0)]
  transfers between devices with their start and end apart: 3 -> 16, of which waited for: 3 -> 11; matrix products, arithmetic and copies ran while one was open for 3% -> 5% of each run, Pallas kernels for 0% -> 9%
where the time goes in v2:
time: 318 us; the launch traced here: 313 us
  waiting for transfers between devices  119 us (37%)
  Pallas kernels  69.9 us (22%)
  blocking collectives  55.4 us (17%)
  starting transfers between devices  38.4 us (12%)
  other arithmetic  16 us (5%)
  local copies, waits for them, and re-layouts  13.1 us (4%)
    all_to_all x6, waiting for transfers between devices, summed(): return lax.all_to_all(part, axis, 0, 0, tiled=True).astype(WIDE).sum(0)  76.8 us
    all_to_all x2, blocking collectives, spread(): lax.all_to_all(jnp.broadcast_to(part[None], (count,) + part.shape), axis,...  55.4 us
    all_to_all x2, waiting for transfers between devices, spread(): lax.all_to_all(jnp.broadcast_to(part[None], (count,) + part.shape), axis,...  36.4 us
    all_to_all x6, starting transfers between devices, summed(): return lax.all_to_all(part, axis, 0, 0, tiled=True).astype(WIDE).sum(0)  23.3 us
    pallas_call x1, Pallas kernels, local(): run_feed_both(core, after_two, g, rows, own_f, oth_f)  14.8 us
    pallas_call x1, Pallas kernels, local(): run_cross_back(core, grad_two, after_one, m, rows, own_a, oth_a, *kept_two)  13.9 us
    pallas_call x1, Pallas kernels, local(): run_self_back(core, grad_one, x, rows, own_a, oth_a, *kept_one)  12.7 us
    pallas_call x1, Pallas kernels, local(): run_cross_forward(core, after_one, m, rows, own_a, oth_a)  11 us
  transfers between devices with their start and end apart: 16, of which 11 were waited for; matrix products, arithmetic and copies ran while one was open for 5% of the time, Pallas kernels for 9%

profile of v2, /device:TPU:2, one launch (start us, length us, event | category | flops | bytes accessed | tf_op | source)
XLA Modules:
  0.0 313.5 jit_solution(14969236598117424850)
XLA Ops:
  0.7 0.7 convert_element_type.64
  1.3 1.0 copy.28
  2.4 0.3 dynamic_update_slice.5
  2.7 0.1 pad_maximum_fusion.3
  2.8 2.4 collective-permute-start
  5.2 3.0 collective-permute-done
  8.1 0.1 slice.48
  8.3 0.7 dynamic-slice_add_fusion
  9.0 0.2 add.63
  9.2 0.1 pad_maximum_fusion.4
  9.3 0.1 copy.29
  9.5 27.7 %all_to_all.55 = bf16[8,80,512]{2,1,0:T(8,128)(2,1)S(1)} all-to-all(bf16[8,80,512]{2,1,0:T(8,128)(2,1)S(1)} %broadcast_in_dim.19), channel_id=1, replica_groups=mesh['xlo'=2,'z'=8,'y'=4,'core'=2,'xhi'=2] {'z'}, dimensions={0} | all-to-all | bytes 1310720 | tf_op jit(solution)/shard_map/all_to_all | solution.py:372
  37.3 0.8 broadcast_in_dim.21
  38.1 3.5 %all-to-all-start.2 = ((bf16[8,64,512]{2,1,0:T(8,128)(2,1)}), bf16[8,64,512]{2,1,0:T(8,128)(2,1)S(1)}, u32[]{:S(2)}, u32[]{:S(2)}) async-start(bf16[8,64,512]{2,1,0:T(8,128)(2,1)} %broadcast_in_dim.21), calls=%async_computation.2 | async-start | bytes 1048576 | tf_op jit(solution)/shard_map/all_to_all | solution.py:372
  41.7 14.9 %all-to-all-done.2 = bf16[8,64,512]{2,1,0:T(8,128)(2,1)S(1)} async-done(((bf16[8,64,512]{2,1,0:T(8,128)(2,1)}), bf16[8,64,512]{2,1,0:T(8,128)(2,1)S(1)}, u32[]{:S(2)}, u32[]{:S(2)}) %all-to-all-start.2) | async-done | bytes 524320 | tf_op jit(solution)/shard_map/all_to_all | solution.py:372
  56.7 0.2 broadcast_in_dim.20
  56.9 27.7 %all_to_all.56.own = bf16[4,528,512]{2,1,0:T(8,128)(2,1)S(1)} all-to-all(bf16[4,528,512]{2,1,0:T(8,128)(2,1)S(1)} %broadcast_in_dim.20), channel_id=1, replica_groups=mesh['xlo'=2,'z'=8,'y'=4,'core'=2,'xhi'=2] {'y'}, dimensions={0} | all-to-all | bytes 4325376 | tf_op jit(solution)/shard_map/all_to_all | solution.py:372
  84.6 1.6 broadcast_in_dim.23
  86.2 4.5 %all-to-all-start.3 = ((bf16[4,512,512]{2,1,0:T(8,128)(2,1)}), bf16[4,512,512]{2,1,0:T(8,128)(2,1)}, u32[]{:S(2)}, u32[]{:S(2)}) async-start(bf16[4,512,512]{2,1,0:T(8,128)(2,1)} %broadcast_in_dim.23), calls=%async_computation.3 | async-start | bytes 4194304 | tf_op jit(solution)/shard_map/all_to_all | solution.py:372
  90.8 21.5 %all-to-all-done.3.own = bf16[4,512,512]{2,1,0:T(8,128)(2,1)} async-done(((bf16[4,512,512]{2,1,0:T(8,128)(2,1)}), bf16[4,512,512]{2,1,0:T(8,128)(2,1)}, u32[]{:S(2)}, u32[]{:S(2)}) %all-to-all-start.3) | async-done | bytes 2097184 | tf_op jit(solution)/shard_map/all_to_all | solution.py:372
  112.2 0.2 collective-permute-start.2
  112.4 10.8 %self_forward.1 = (bf16[512,512]{1,0:T(8,128)(2,1)}, bf16[512,512]{1,0:T(8,128)(2,1)}, bf16[512,512]{1,0:T(8,128)(2,1)}, bf16[16,256,256]{2,1,0:T(8,128)(2,1)}, ...) custom-call(s32[1]{0:T(128)} %bitcast.core_ref, bf16[512,512]{1,0:T(8,128)(2,1)} %bitcast.14, ...), custom_call_target="tpu_custom_call" | custom-call | flops 1400000000 | bytes 8388608 | tf_op jit(solution)/shard_map/self_forward/pallas_call | solution.py:420
  123.2 11.0 %cross_forward.1 = (bf16[512,512]{1,0:T(8,128)(2,1)}, bf16[512,512]{1,0:T(8,128)(2,1)}, bf16[512,512]{1,0:T(8,128)(2,1)}, bf16[16,256,256]{2,1,0:T(8,128)(2,1)},...) custom-call(s32[1]{0:T(128)} %bitcast.core_ref, f32[512,512]{1,0:T(8,128)} %get-tuple-element.44.x_ref, ...), custom_call_target="tpu_custom_call" | custom-call | flops 1400000000 | bytes 8388608 | tf_op jit(solution)/shard_map/cross_forward/pallas_call | solution.py:421
  134.3 1.3 copy-done.11
  135.6 14.8 %feed_both.1 = (bf16[512,512]{1,0:T(8,128)(2,1)}, f32[512,512]{1,0:T(8,128)}, bf16[4,8,64,512]{3,2,1,0:T(8,128)(2,1)}, bf16[4,8,64,512]{3,2,1,0:T(8,128)(2,1)}, f32[8,512]{1,0:T(8,128)}) custom-call(s32[1]{0:T(128)} %bitcast.core_ref, f32[512,512]{1,0:T(8,128)} %get-tuple-element.46.x_ref, bf16[512,512]{1,0:T(8,128)(2,1)} %bitcast.22, ...), custom_call_target="tpu_custom_call" | custom-call | flops 6600000000 | bytes 8388608 | tf_op jit(solution)/shard_map/feed_both/pallas_call | solution.py:422
  150.5 13.9 %cross_back.1 = (f32[512,512]{1,0:T(8,128)}, bf16[512,512]{1,0:T(8,128)(2,1)}, bf16[512,512]{1,0:T(8,128)(2,1)}, bf16[4,4,64,512]{3,2,1,0:T(8,128)(2,1)}, bf16[4...) custom-call(s32[1]{0:T(128)} %bitcast.core_ref, f32[512,512]{1,0:T(8,128)} %get-tuple-element.49.d_ref, ...), custom_call_target="tpu_custom_call" | custom-call | flops 2400000000 | bytes 8388608 | tf_op jit(solution)/shard_map/cross_back/pallas_call | solution.py:426
  164.3 12.7 %self_back.1 = (bf16[512,512]{1,0:T(8,128)(2,1)}, bf16[512,512]{1,0:T(8,128)(2,1)}, bf16[512,512]{1,0:T(8,128)(2,1)}, bf16[4,4,64,512]{3,2,1,0:T(8,128)(2,1)}, bf16[4,4,64,512]{3,2,1,0:T(8,128)(2,1)}) custom-call(s32[1]{0:T(128)} %bitcast.core_ref, f32[512,512]{1,0:T(8,128)} %get-tuple-element.55.d_ref, bf16[512,512]{1,0:T(8,128)(2,1)} %bitcast.15, ...), custom_call_target="tpu_custom_call" | custom-call | flops 2400000000 | bytes 8388608 | tf_op jit(solution)/shard_map/self_back/pallas_call | solution.py:431
  177.0 0.6 collective-permute-start.3
  177.8 0.4 collective-permute-start.4
  178.2 6.7 %last_back.1 = (f32[512,512]{1,0:T(8,128)}, f32[512,512]{1,0:T(8,128)}, f32[8,512]{1,0:T(8,128)}) custom-call(s32[1]{0:T(128)} %bitcast.core_ref, f32[512,512]{1,0:T(8,128)} %get-tuple-element.55.d_ref, bf16[512,512]{1,0:T(8,128)(2,1)} %bitcast.16, f32[8,512]{1,0:T(8,128)} %get-tuple-element.45.n_ref, bf16[4,528,512]{2,1,0:T(8,128)(2,1)} %copy-done, ...), custom_call_target="tpu_custom_call" | custom-call | flops 1400000000 | bytes 8388608 | tf_op jit(solution)/shard_map/last_back/pallas_call | solution.py:437
  184.9 0.7 slice.64
  185.6 0.7 slice.63
  186.3 0.7 slice.62
  187.1 0.1 collective-permute-start.5
  187.3 1.1 collective-permute-done.5
  188.4 0.6 broadcast_in_dim.50
  189.1 3.3 %all-to-all-start.6 = ((bf16[4,16,512]{2,1,0:T(8,128)(2,1)}), bf16[4,16,512]{2,1,0:T(8,128)(2,1)S(1)}, u32[]{:S(2)}, u32[]{:S(2)}) async-start(bf16[4,16,512]{2,1,0:T(8,128)(2,1)} %broadcast_in_dim.50), calls=%async_computation.6 | async-start | bytes 131072 | tf_op jit(solution)/shard_map/all_to_all | solution.py:445
  192.4 1.0 copy-done.4
  193.4 2.6 add_convert_fusion.2
  196.0 2.0 all-to-all-done.6
  197.9 3.5 %all-to-all-start.4 = ((bf16[4,4,64,512]{3,2,1,0:T(8,128)(2,1)}), bf16[4,4,64,512]{3,2,1,0:T(8,128)(2,1)S(1)}, u32[]{:S(2)}, u32[]{:S(2)}) async-start(bf16[4,4,64,512]{3,2,1,0:T(8,128)(2,1)} %add_convert_fusion.2), calls=%async_computation.4 | async-start | bytes 2097152 | tf_op jit(solution)/shard_map/all_to_all | solution.py:378
  201.5 1.3 add_convert_fusion.1
  202.8 13.2 %all-to-all-done.4 = bf16[4,4,64,512]{3,2,1,0:T(8,128)(2,1)S(1)} async-done(((bf16[4,4,64,512]{3,2,1,0:T(8,128)(2,1)}), bf16[4,4,64,512]{3,2,1,0:T(8,128)(2,1)S(1)}, u32[]{:S(2)}, u32[]{:S(2)}) %all-to-all-start.4) | async-done | bytes 1048608 | tf_op jit(solution)/shard_map/all_to_all | solution.py:378
  216.0 3.5 %all-to-all-start.5 = ((bf16[4,4,64,512]{3,2,1,0:T(8,128)(2,1)}), bf16[4,4,64,512]{3,2,1,0:T(8,128)(2,1)S(1)}, u32[]{:S(2)}, u32[]{:S(2)}) async-start(bf16[4,4,64,512]{3,2,1,0:T(8,128)(2,1)} %add_convert_fusion.1), calls=%async_computation.5 | async-start | bytes 2097152 | tf_op jit(solution)/shard_map/all_to_all | solution.py:378
  219.5 4.5 %add_convert_fusion = bf16[4,8,64,512]{3,2,1,0:T(8,128)(2,1)} fusion(bf16[4,8,64,512]{3,2,1,0:T(8,128)(2,1)} %collective-permute-done.6, bf16[4,8,64,512]{3,2,1,0:T(8,128)(2,1)} %get-tuple-element.75), kind=kLoop, calls=%fused_computation | loop fusion | flops 4194304 | bytes 6291456 | tf_op jit(solution)/shard_map/convert_element_type | solution.py:382
  224.0 9.1 %all-to-all-done.5 = bf16[4,4,64,512]{3,2,1,0:T(8,128)(2,1)S(1)} async-done(((bf16[4,4,64,512]{3,2,1,0:T(8,128)(2,1)}), bf16[4,4,64,512]{3,2,1,0:T(8,128)(2,1)S(1)}, u32[]{:S(2)}, u32[]{:S(2)}) %all-to-all-start.5) | async-done | bytes 1048608 | tf_op jit(solution)/shard_map/all_to_all | solution.py:378
  233.1 1.0 copy-done.1
  234.1 3.6 %all-to-all-start.8 = ((bf16[4,8,64,512]{3,2,1,0:T(8,128)(2,1)}), bf16[4,8,64,512]{3,2,1,0:T(8,128)(2,1)S(1)}, u32[]{:S(2)}, u32[]{:S(2)}) async-start(bf16[4,8,64,512]{3,2,1,0:T(8,128)(2,1)} %add_convert_fusion), calls=%async_computation.8 | async-start | bytes 4194304 | tf_op jit(solution)/shard_map/all_to_all | solution.py:378
  237.7 0.2 reduce.5
  238.0 1.4 reduce.6
  239.4 0.9 pad_maximum_fusion
  240.3 21.0 %all-to-all-done.8 = bf16[4,8,64,512]{3,2,1,0:T(8,128)(2,1)S(1)} async-done(((bf16[4,8,64,512]{3,2,1,0:T(8,128)(2,1)}), bf16[4,8,64,512]{3,2,1,0:T(8,128)(2,1)S(1)}, u32[]{:S(2)}, u32[]{:S(2)}) %all-to-all-start.8) | async-done | bytes 2097184 | tf_op jit(solution)/shard_map/all_to_all | solution.py:378
  261.3 4.3 %all-to-all-start.7 = ((bf16[8,80,512]{2,1,0:T(8,128)(2,1)}), bf16[8,80,512]{2,1,0:T(8,128)(2,1)S(1)}, u32[]{:S(2)}, u32[]{:S(2)}) async-start(bf16[8,80,512]{2,1,0:T(8,128)(2,1)} %pad_maximum_fusion), calls=%async_computation.7 | async-start | bytes 1310720 | tf_op jit(solution)/shard_map/all_to_all | solution.py:378
  265.7 1.3 reduce_sum.92
  267.0 15.2 %all-to-all-done.7 = bf16[8,80,512]{2,1,0:T(8,128)(2,1)S(1)} async-done(((bf16[8,80,512]{2,1,0:T(8,128)(2,1)}), bf16[8,80,512]{2,1,0:T(8,128)(2,1)S(1)}, u32[]{:S(2)}, u32[]{:S(2)}) %all-to-all-start.7) | async-done | bytes 655392 | tf_op jit(solution)/shard_map/all_to_all | solution.py:378
  282.1 3.5 %all-to-all-start.9 = ((bf16[8,64,512]{2,1,0:T(8,128)(2,1)}), bf16[8,64,512]{2,1,0:T(8,128)(2,1)S(1)}, u32[]{:S(2)}, u32[]{:S(2)}) async-start(bf16[8,64,512]{2,1,0:T(8,128)(2,1)} %reduce_sum.92), calls=%async_computation.9 | async-start | bytes 1048576 | tf_op jit(solution)/shard_map/all_to_all | solution.py:378
  285.7 13.1 %all-to-all-done.9 = bf16[8,64,512]{2,1,0:T(8,128)(2,1)S(1)} async-done(((bf16[8,64,512]{2,1,0:T(8,128)(2,1)}), bf16[8,64,512]{2,1,0:T(8,128)(2,1)S(1)}, u32[]{:S(2)}, u32[]{:S(2)}) %all-to-all-start.9) | async-done | bytes 524320 | tf_op jit(solution)/shard_map/all_to_all | solution.py:378
  298.9 0.8 pad_maximum_fusion.2
  299.7 4.8 %all-to-all-start.10 = ((bf16[4,80,512]{2,1,0:T(8,128)(2,1)}), bf16[4,80,512]{2,1,0:T(8,128)(2,1)S(1)}, u32[]{:S(2)}, u32[]{:S(2)}) async-start(bf16[4,80,512]{2,1,0:T(8,128)(2,1)} %pad_maximum_fusion.2), calls=%async_computation.10 | async-start | bytes 655360 | tf_op jit(solution)/shard_map/all_to_all | solution.py:378
  304.8 5.3 %all-to-all-done.10 = bf16[4,80,512]{2,1,0:T(8,128)(2,1)S(1)} async-done(((bf16[4,80,512]{2,1,0:T(8,128)(2,1)}), bf16[4,80,512]{2,1,0:T(8,128)(2,1)S(1)}, u32[]{:S(2)}, u32[]{:S(2)}) %all-to-all-start.10) | async-done | bytes 327712 | tf_op jit(solution)/shard_map/all_to_all | solution.py:378
  310.2 0.7 copy.35
  310.9 0.7 copy.36
  311.6 0.7 copy.37
  312.3 0.8 multiply_subtract_fusion
  (52 shorter events, 1.4 us)
Async XLA Ops:
  2.8 5.3 %collective-permute-start = (bf16[80,512]{0,1:T(8,128)(2,1)S(1)}, bf16[80,512]{0,1:T(8,128)(2,1)S(1)}, u32[]{:S(2)}, u32[]{:S(2)}) collective-permute-start(bf16[80,512]{0,1:T(8,128)(2,1)S(1)} %pad_maximum_fusion.3), channel_id=1, source_target_pairs={{0,128},{128,0},{1,129},{129,1},{2,130},{130,2},{3,131},{131,3},{4... | collective-permute-start | bytes 245768 | tf_op jit(solution)/shard_map/ppermute | solution.py:368
  38.1 18.6 %all-to-all-start.2 = ((bf16[8,64,512]{2,1,0:T(8,128)(2,1)}), bf16[8,64,512]{2,1,0:T(8,128)(2,1)S(1)}, u32[]{:S(2)}, u32[]{:S(2)}) async-start(bf16[8,64,512]{2,1,0:T(8,128)(2,1)} %broadcast_in_dim.21), calls=%async_computation.2 | async-start | bytes 1048576 | tf_op jit(solution)/shard_map/all_to_all | solution.py:372
  84.6 6.1 %copy-start = (bf16[4,528,512]{2,1,0:T(8,128)(2,1)}, bf16[4,528,512]{2,1,0:T(8,128)(2,1)S(1)}, u32[]{:S(2)}) copy-start(bf16[4,528,512]{2,1,0:T(8,128)(2,1)S(1)} %all_to_all.56.own) | copy-start | bytes 6488068
  86.2 26.1 %all-to-all-start.3 = ((bf16[4,512,512]{2,1,0:T(8,128)(2,1)}), bf16[4,512,512]{2,1,0:T(8,128)(2,1)}, u32[]{:S(2)}, u32[]{:S(2)}) async-start(bf16[4,512,512]{2,1,0:T(8,128)(2,1)} %broadcast_in_dim.23), calls=%async_computation.3 | async-start | bytes 4194304 | tf_op jit(solution)/shard_map/all_to_all | solution.py:372
  90.7 21.7 %collective-permute-start.1 = (bf16[4,528,512]{2,1,0:T(8,128)(2,1)S(1)}, bf16[4,528,512]{2,1,0:T(8,128)(2,1)}, u32[]{:S(2)}, u32[]{:S(2)}) collective-permute-start(bf16[4,528,512]{2,1,0:T(8,128)(2,1)S(1)} %all_to_all.56.own), channel_id=1, source_target_pairs={{0,2},{2,0},{1,3},{3,1},{4,6},{6,4},{5,7},{7,5},{8,10},{10,8},{9,1... | collective-permute-start | bytes 6488072 | tf_op jit(solution)/shard_map/ppermute | solution.py:368
  112.2 22.0 %collective-permute-start.2 = (bf16[4,512,512]{2,1,0:T(8,128)(2,1)}, bf16[4,512,512]{2,1,0:T(8,128)(2,1)S(1)}, u32[]{:S(2)}, u32[]{:S(2)}) collective-permute-start(bf16[4,512,512]{2,1,0:T(8,128)(2,1)} %all-to-all-done.3.own), channel_id=1, source_target_pairs={{0,2},{2,0},{1,3},{3,1},{4,6},{6,4},{5,7},{7,5},{8,10},{10,8},{9,1... | collective-permute-start | bytes 6291464 | tf_op jit(solution)/shard_map/ppermute | solution.py:368
  134.3 1.3 copy-start.11
  177.0 15.4 %collective-permute-start.3 = (bf16[4,4,64,512]{3,2,1,0:T(8,128)(2,1)}, bf16[4,4,64,512]{3,2,1,0:T(8,128)(2,1)S(1)}, u32[]{:S(2)}, u32[]{:S(2)}) collective-permute-start(bf16[4,4,64,512]{3,2,1,0:T(8,128)(2,1)} %get-tuple-element.69), channel_id=1, source_target_pairs={{0,2},{2,0},{1,3},{3,1},{4,6},{6,4},{5,7},{7,5},{8,10},{10,8},{9,1... | collective-permute-start | bytes 3145736 | tf_op jit(solution)/shard_map/ppermute | solution.py:368
  177.6 41.9 %collective-permute-start.6 = (bf16[4,8,64,512]{3,2,1,0:T(8,128)(2,1)}, bf16[4,8,64,512]{3,2,1,0:T(8,128)(2,1)}, u32[]{:S(2)}, u32[]{:S(2)}) collective-permute-start(bf16[4,8,64,512]{3,2,1,0:T(8,128)(2,1)} %get-tuple-element.76), channel_id=1, source_target_pairs={{0,2},{2,0},{1,3},{3,1},{4,6},{6,4},{5,7},{7,5},{8,10},{10,8},{9,1... | collective-permute-start | bytes 6291464 | tf_op jit(solution)/shard_map/ppermute | solution.py:368
  177.8 23.7 %collective-permute-start.4 = (bf16[4,4,64,512]{3,2,1,0:T(8,128)(2,1)}, bf16[4,4,64,512]{3,2,1,0:T(8,128)(2,1)S(1)}, u32[]{:S(2)}, u32[]{:S(2)}) collective-permute-start(bf16[4,4,64,512]{3,2,1,0:T(8,128)(2,1)} %get-tuple-element.71), channel_id=1, source_target_pairs={{0,2},{2,0},{1,3},{3,1},{4,6},{6,4},{5,7},{7,5},{8,10},{10,8},{9,1... | collective-permute-start | bytes 3145736 | tf_op jit(solution)/shard_map/ppermute | solution.py:368
  178.2 15.2 %copy-start.3 = (bf16[4,4,64,512]{3,2,1,0:T(8,128)(2,1)S(1)}, bf16[4,4,64,512]{3,2,1,0:T(8,128)(2,1)}, u32[]{:S(2)}) copy-start(bf16[4,4,64,512]{3,2,1,0:T(8,128)(2,1)} %get-tuple-element.68) | copy-start | bytes 3145732
  187.1 1.2 collective-permute-start.5
  189.1 8.9 %all-to-all-start.6 = ((bf16[4,16,512]{2,1,0:T(8,128)(2,1)}), bf16[4,16,512]{2,1,0:T(8,128)(2,1)S(1)}, u32[]{:S(2)}, u32[]{:S(2)}) async-start(bf16[4,16,512]{2,1,0:T(8,128)(2,1)} %broadcast_in_dim.50), calls=%async_computation.6 | async-start | bytes 131072 | tf_op jit(solution)/shard_map/all_to_all | solution.py:445
  192.4 1.0 copy-start.4
  193.4 8.1 %copy-start.2 = (bf16[4,4,64,512]{3,2,1,0:T(8,128)(2,1)S(1)}, bf16[4,4,64,512]{3,2,1,0:T(8,128)(2,1)}, u32[]{:S(2)}) copy-start(bf16[4,4,64,512]{3,2,1,0:T(8,128)(2,1)} %get-tuple-element.70) | copy-start | bytes 3145732
  197.9 18.0 %all-to-all-start.4 = ((bf16[4,4,64,512]{3,2,1,0:T(8,128)(2,1)}), bf16[4,4,64,512]{3,2,1,0:T(8,128)(2,1)S(1)}, u32[]{:S(2)}, u32[]{:S(2)}) async-start(bf16[4,4,64,512]{3,2,1,0:T(8,128)(2,1)} %add_convert_fusion.2), calls=%async_computation.4 | async-start | bytes 2097152 | tf_op jit(solution)/shard_map/all_to_all | solution.py:378
  216.0 17.1 %all-to-all-start.5 = ((bf16[4,4,64,512]{3,2,1,0:T(8,128)(2,1)}), bf16[4,4,64,512]{3,2,1,0:T(8,128)(2,1)S(1)}, u32[]{:S(2)}, u32[]{:S(2)}) async-start(bf16[4,4,64,512]{3,2,1,0:T(8,128)(2,1)} %add_convert_fusion.1), calls=%async_computation.5 | async-start | bytes 2097152 | tf_op jit(solution)/shard_map/all_to_all | solution.py:378
  233.1 1.0 copy-start.1
  234.1 27.2 %all-to-all-start.8 = ((bf16[4,8,64,512]{3,2,1,0:T(8,128)(2,1)}), bf16[4,8,64,512]{3,2,1,0:T(8,128)(2,1)S(1)}, u32[]{:S(2)}, u32[]{:S(2)}) async-start(bf16[4,8,64,512]{3,2,1,0:T(8,128)(2,1)} %add_convert_fusion), calls=%async_computation.8 | async-start | bytes 4194304 | tf_op jit(solution)/shard_map/all_to_all | solution.py:378
  261.3 20.8 %all-to-all-start.7 = ((bf16[8,80,512]{2,1,0:T(8,128)(2,1)}), bf16[8,80,512]{2,1,0:T(8,128)(2,1)S(1)}, u32[]{:S(2)}, u32[]{:S(2)}) async-start(bf16[8,80,512]{2,1,0:T(8,128)(2,1)} %pad_maximum_fusion), calls=%async_computation.7 | async-start | bytes 1310720 | tf_op jit(solution)/shard_map/all_to_all | solution.py:378
  266.9 37.6 %copy-start.8 = (f32[6,4]{0,1:T(4,128)S(1)}, f32[6,4]{0,1:T(4,128)}, u32[]{:S(2)}) copy-start(f32[6,4]{0,1:T(4,128)} %param.15) | copy-start | bytes 292
  266.9 37.7 %copy-start.9 = (f32[6,4]{0,1:T(4,128)S(1)}, f32[6,4]{0,1:T(4,128)}, u32[]{:S(2)}) copy-start(f32[6,4]{0,1:T(4,128)} %param.17) | copy-start | bytes 292
  266.9 37.8 %copy-start.10 = (f32[6,4]{0,1:T(4,128)S(1)}, f32[6,4]{0,1:T(4,128)}, u32[]{:S(2)}) copy-start(f32[6,4]{0,1:T(4,128)} %param.16) | copy-start | bytes 292
  266.9 45.3 %copy-start.5 = (f32[64,512]{1,0:T(8,128)S(1)}, f32[64,512]{1,0:T(8,128)}, u32[]{:S(2)}) copy-start(f32[64,512]{1,0:T(8,128)} %param.12) | copy-start | bytes 393220
  267.0 45.3 %copy-start.6 = (f32[64,512]{1,0:T(8,128)S(1)}, f32[64,512]{1,0:T(8,128)}, u32[]{:S(2)}) copy-start(f32[64,512]{1,0:T(8,128)} %param.13) | copy-start | bytes 393220
  267.0 45.3 %copy-start.7 = (f32[64,512]{1,0:T(8,128)S(1)}, f32[64,512]{1,0:T(8,128)}, u32[]{:S(2)}) copy-start(f32[64,512]{1,0:T(8,128)} %param.14) | copy-start | bytes 393220
  282.1 16.7 %all-to-all-start.9 = ((bf16[8,64,512]{2,1,0:T(8,128)(2,1)}), bf16[8,64,512]{2,1,0:T(8,128)(2,1)S(1)}, u32[]{:S(2)}, u32[]{:S(2)}) async-start(bf16[8,64,512]{2,1,0:T(8,128)(2,1)} %reduce_sum.92), calls=%async_computation.9 | async-start | bytes 1048576 | tf_op jit(solution)/shard_map/all_to_all | solution.py:378
  299.7 10.4 %all-to-all-start.10 = ((bf16[4,80,512]{2,1,0:T(8,128)(2,1)}), bf16[4,80,512]{2,1,0:T(8,128)(2,1)S(1)}, u32[]{:S(2)}, u32[]{:S(2)}) async-start(bf16[4,80,512]{2,1,0:T(8,128)(2,1)} %pad_maximum_fusion.2), calls=%async_computation.10 | async-start | bytes 655360 | tf_op jit(solution)/shard_map/all_to_all | solution.py:378
